TPU v7x, 256 devices: a whole 4x4x8 slice. The times are simulated.
256 devices in a mesh: node: 16 (over y_hi, x, core), replica: 16 (over y_lo, z).
Axes of the slice: x: 4, y: 4 (y_hi: 2, y_lo: 2; y = y_hi * 2 + y_lo), z: 8, core: 2. Of those that a mesh axis runs over, the one named last changes fastest.
Arguments:
- hidden_act: bfloat16 [196608, 1024], P(('node', 'replica')), may hold values from -24 to 24
- out_grad: bfloat16 [196608, 3584], P(('node', 'replica')), may hold values from -0.023925781 to 0.023925781
- tile_list: int32 [16, 16, 2, 6], P('node', 'replica'), may hold values from 0 to 5, as said below
- tile_count: int32 [16, 16, 2], P('node', 'replica'), may hold values from 1 to 5, as said below
- momentum: float32 [2, 1024, 3584], P(None, 'node'), may hold values from -6 to 6
- weight: bfloat16 [2, 1024, 3584], P(None, 'node'), may hold values from -0.1875 to 0.1875
- next_act: bfloat16 [2, 16384, 1024], P(None, ('node', 'replica')), may hold values from -6 to 6
Outputs:
- new_momentum: float32 [2, 1024, 3584], P(None, 'node')
- next_out: bfloat16 [2, 16384, 3584], P(None, ('node', 'replica'))
Inputs may be any that keep to these rules, and one draw needn't show every extreme that they name: `tile_list`: for each device and expert the first tile_count entries name distinct tiles of that device; the two experts' named tiles together cover every tile of the device exactly once; entries past the count are tile numbers without meaning. `tile_count`: the counts of one device sum to 6.
All inputs are finite; a program needn't handle non-finite values.
Results may differ from a plain program's by a relative error of at most 0.022.
Values may be sent and summed in bfloat16 or wider, within the bound.
No kernel may reach another device: no remote copies, remote signals or barrier semaphores. Data moves between devices by JAX's collectives and lax.ppermute only.
A program may use at most 128 MiB of HBM per device.

v0:
```python
import jax
import jax.numpy as jnp
from jax import lax
from jax.sharding import PartitionSpec as P

BUCKETS = 2


momentum_decay = 0.9
learning_rate = 0.01


def bucket_masks(route_lists, route_counts, tile_rows):
    tile_total = route_lists.shape[-1]
    tile_slots = jnp.arange(tile_total, dtype=jnp.int32)
    live_slot = tile_slots[None, :] < route_counts[:, None]
    named_tile = (route_lists[:, :, None] == tile_slots[None, None, :]) & live_slot[:, :, None]
    owned_tile = jnp.any(named_tile, axis=1)
    return jnp.repeat(owned_tile, tile_rows, axis=1)


def local(hidden_act, out_grad, tile_list, tile_count, momentum, weight, next_act):
    tile_total = tile_list.shape[-1]
    row_count = hidden_act.shape[0]
    hidden_width = hidden_act.shape[1]
    feature_width = out_grad.shape[1]
    route_lists = tile_list.reshape(BUCKETS, tile_total)
    route_counts = tile_count.reshape(BUCKETS)
    owned_rows = bucket_masks(route_lists, route_counts, row_count // tile_total)
    node_count = lax.axis_size("node")
    momentum_out = []
    product_out = []
    for bucket in range(BUCKETS):
        masked = jnp.where(owned_rows[bucket][:, None], out_grad, jnp.zeros_like(out_grad))

        def partial_rows(first_row, row_span, masked=masked):
            return lax.dot_general(
                hidden_act, masked, (((0,), (0,)), ((), ())), preferred_element_type=jnp.float32
            )

        node_share = lax.psum_scatter(
            partial_rows(jnp.int32(0), hidden_width // node_count * lax.axis_size("node")).astype(
                jnp.bfloat16
            ),
            "node",
            scatter_dimension=0,
            tiled=True,
        )
        grad_share = lax.psum(node_share, "replica").astype(jnp.float32)
        updated = momentum_decay * momentum[bucket] + grad_share
        new_weight = (weight[bucket].astype(jnp.float32) - learning_rate * updated).astype(
            jnp.bfloat16
        )
        next_rows = next_act[bucket]

        def accumulate(running, block_rows, first_row, next_rows=next_rows):
            return jnp.dot(next_rows, block_rows, preferred_element_type=jnp.float32)

        zero_out = jnp.zeros((next_rows.shape[0], feature_width), jnp.float32)
        product = accumulate(
            zero_out, lax.all_gather(new_weight, "node", axis=0, tiled=True), jnp.int32(0)
        )
        momentum_out.append(updated)
        product_out.append(product.astype(jnp.bfloat16))
    return (jnp.stack(momentum_out), jnp.stack(product_out))


def solution(mesh):
    in_specs = (
        P(("node", "replica"), None),
        P(("node", "replica"), None),
        P("node", "replica", None, None),
        P("node", "replica", None),
        P(None, "node", None),
        P(None, "node", None),
        P(None, ("node", "replica"), None),
    )
    out_specs = (P(None, "node", None), P(None, ("node", "replica"), None))
    return jax.shard_map(local, mesh=mesh, in_specs=in_specs, out_specs=out_specs, check_vma=False)
```

profile of v0, /device:TPU:1, one launch (start us, length us, event | category | flops | bytes accessed | tf_op | source)
XLA Modules:
  0.0 548.6 jit_solution(10588192035040948556)
XLA Ops:
  8.9 10.8 %fusion = bf16[1024,3584]{0,1:T(8,128)(2,1)} fusion(bf16[768,1024]{1,0:T(8,128)(2,1)S(1)} %copy-done, bf16[768,3584]{1,0:T(8,128)(2,1)} %param.8, pred[768]{0:T(1024)(128)(4,1)S(1)} %get-tuple-element.21), kind=kOutput, calls=%fused_computation.2 | convolution fusion | flops 5643567104 | bytes 14418688 | tf_op jit(solution)/shard_map/dot_general | solution.py:37
  19.7 10.0 %copy.28 = bf16[1024,3584]{1,0:T(8,128)(2,1)} copy(bf16[1024,3584]{0,1:T(8,128)(2,1)} %fusion) | data formatting | bytes 14680064
  29.8 10.9 %fusion.1 = bf16[1024,3584]{0,1:T(8,128)(2,1)} fusion(bf16[768,1024]{1,0:T(8,128)(2,1)S(1)} %copy-done, bf16[768,3584]{1,0:T(8,128)(2,1)} %param.8, pred[768]{0:T(1024)(128)(4,1)S(1)} %get-tuple-element.20), kind=kOutput, calls=%fused_computation.3 | convolution fusion | flops 5643567104 | bytes 14418688 | tf_op jit(solution)/shard_map/dot_general | solution.py:37
  40.7 10.2 %copy.30 = bf16[1024,3584]{1,0:T(8,128)(2,1)} copy(bf16[1024,3584]{0,1:T(8,128)(2,1)} %fusion.1) | data formatting | bytes 14680064
  50.9 1.6 copy-done.3
  52.5 1.1 fusion.22
  53.6 1.8 copy.32
  55.3 78.9 %reduce-scatter.7.cloned.1.call-done = bf16[64,3584]{1,0:T(8,128)(2,1)} async-done(((bf16[1024,3584]{1,0:T(8,128)(2,1)}), bf16[64,3584]{1,0:T(8,128)(2,1)}) %reduce-scatter.7.cloned.1.call-update) | async-done | bytes 458768
  134.3 2.2 copy.29
  136.5 103.7 %reduce-scatter.9.cloned.1.call-done = bf16[64,3584]{1,0:T(8,128)(2,1)} async-done(((bf16[1024,3584]{1,0:T(8,128)(2,1)}), bf16[64,3584]{1,0:T(8,128)(2,1)}) %reduce-scatter.9.cloned.1.call-update) | async-done | bytes 458768
  240.2 2.3 copy.31
  243.1 132.2 %all-reduce.3.cloned.1.call-done = (bf16[64,3584]{0,1:T(8,128)(2,1)}, bf16[64,3584]{0,1:T(8,128)(2,1)}) async-done(((bf16[64,3584]{0,1:T(8,128)(2,1)}, bf16[64,3584]{0,1:T(8,128)(2,1)}), (bf16[64,3584]{0,1:T(8,128)(2,1)}, bf16[64,3584]{0,1:T(8,128)(2,1)})) %all-reduce.3.cloned.1.call-update) | async-done | bytes 917520 | tf_op jit(solution)/shard_map/psum | solution.py:49
  375.3 3.1 fusion.11
  378.4 2.3 copy.24
  381.0 1.8 copy.33
  383.2 3.7 fusion.10
  386.9 2.2 copy.26
  389.2 3.6 pad_maximum_fusion
  392.7 3.5 copy.27
  396.3 65.7 %all-gather.3.cloned.1.call-done = bf16[1024,3584]{1,0:T(8,128)(2,1)} async-done(((bf16[64,3584]{1,0:T(8,128)(2,1)}), bf16[1024,3584]{1,0:T(8,128)(2,1)}) %all-gather.3.cloned.1.call-update) | async-done | bytes 7340048 | tf_op jit(solution)/shard_map/all_gather | solution.py:61
  461.9 4.5 fusion.6
  466.4 70.1 %all-gather.5.cloned.1.call-done = bf16[1024,3584]{1,0:T(8,128)(2,1)} async-done(((bf16[64,3584]{1,0:T(8,128)(2,1)}), bf16[1024,3584]{1,0:T(8,128)(2,1)}) %all-gather.5.cloned.1.call-update) | async-done | bytes 7340048 | tf_op jit(solution)/shard_map/all_gather | solution.py:61
  536.5 4.6 fusion.7
  541.1 1.0 pad_maximum_fusion.1
  (28 shorter events, 3.1 us)
Async XLA Ops:
  7.2 1.8 copy-start
  7.2 127.1 %reduce-scatter.7.cloned.1.call-start = ((), (), s32[]{:S(2)}) async-start(), calls=%async_computation.4 | async-start | bytes 7798784
  29.7 210.5 %reduce-scatter.9.cloned.1.call-start = ((), (), s32[]{:S(2)}) async-start(), calls=%async_computation.5 | async-start | bytes 7798784
  50.9 1.6 copy-start.3
  50.9 324.4 %all-reduce.3.cloned.1.call-start = ((), (), s32[]{:S(2)}) async-start(), calls=%async_computation.6 | async-start | bytes 3670016 | tf_op jit(solution)/shard_map/psum | solution.py:49
  136.5 106.1 %copy-start.4 = (bf16[2,64,3584]{2,1,0:T(8,128)(2,1)S(1)}, bf16[2,64,3584]{2,1,0:T(8,128)(2,1)}, u32[]{:S(2)}) copy-start(bf16[2,64,3584]{2,1,0:T(8,128)(2,1)} %param.12) | copy-start | bytes 2752516
  242.5 219.4 %all-gather.3.cloned.1.call-start = ((), (), s32[]{:S(2)}) async-start(), calls=%async_computation.2 | async-start | bytes 7798784 | tf_op jit(solution)/shard_map/all_gather | solution.py:61
  378.4 2.6 copy-start.2
  380.7 155.8 %all-gather.5.cloned.1.call-start = ((), (), s32[]{:S(2)}) async-start(), calls=%async_computation.3 | async-start | bytes 7798784 | tf_op jit(solution)/shard_map/all_gather | solution.py:61
  392.7 69.2 %copy-start.5 = (bf16[2,64,1024]{2,1,0:T(8,128)(2,1)S(1)}, bf16[2,64,1024]{2,1,0:T(8,128)(2,1)}, u32[]{:S(2)}) copy-start(bf16[2,64,1024]{2,1,0:T(8,128)(2,1)} %param.13) | copy-start | bytes 786436
  536.5 5.6 %copy-start.1 = (bf16[768,1024]{1,0:T(8,128)(2,1)S(1)}, bf16[768,1024]{1,0:T(8,128)(2,1)}, u32[]{:S(2)}) copy-start(bf16[768,1024]{1,0:T(8,128)(2,1)} %param.7) | copy-start | bytes 4718596
Sparse Core Ops, SparseCore 0:
  29.9 104.3 reduce-scatter.6
  139.4 100.7 reduce-scatter.8
  243.5 131.6 all-reduce.2
  380.8 81.0 all-gather.2
  464.9 71.5 all-gather.4
where the time goes:
time: 550 us; the launch traced here: 549 us
  waiting for transfers between devices  451 us (82%)
  local copies, waits for them, and re-layouts  40 us (7%)
  matrix products  30.7 us (6%)
  between operations  13.8 us (3%)
  other arithmetic  13 us (2%)
    unnamed x7, waiting for transfers between devices  183 us
    all_gather x2, waiting for transfers between devices, local(): lax.all_gather(new_weight, 'node', axis=0, tiled=True)  136 us
    psum x1, waiting for transfers between devices, local(): grad_share = lax.psum(node_share, 'replica').astype(jnp.float32)  132 us
    unnamed x21, local copies, waits for them, and re-layouts  34.2 us
    dot_general x2, matrix products, partial_rows(): lax.dot_general(hidden_act, masked, (((0,), (0,)), ((), ())), preferred_e...  21.7 us
  transfers between devices with their start and end apart: 5, of which 5 were waited for; matrix products, arithmetic and copies ran while one was open for 8% of the time, Pallas kernels for 0%

commit v1 on v0

v1 whole, which is shorter than its diff:
```python
import functools

import jax
import jax.numpy as jnp
from jax import lax
from jax.experimental import pallas as pl
from jax.experimental.pallas import tpu as pltpu
from jax.sharding import PartitionSpec as P

BUCKETS = 2
TILE = 128
TILES = 6
AXES = ("y_hi", "x", "core", "y_lo", "z_hi", "z_lo")
GROUP = ("y_hi", "y_lo", "z_lo")
F32 = jnp.float32
BF16 = jnp.bfloat16

momentum_decay = 0.9
learning_rate = 0.01

NX, NY, NZ = 4, 4, 8
FEATURES = 3584
QUARTER = 896
CHUNK = 128
HALF = 512


def flat(yh, x, c, yl, z):
    return ((yh * NX + x) * 2 + c) * 16 + yl * NZ + z


def send(value, move):
    pairs = []
    for yh in range(2):
        for x in range(NX):
            for c in range(2):
                for yl in range(2):
                    for z in range(NZ):
                        here = flat(yh, x, c, yl, z)
                        pairs.append((here, flat(*move(yh, x, c, yl, z))))
    return lax.ppermute(value, AXES, pairs)


def shift_x(k):
    return lambda yh, x, c, yl, z: (yh, (x + k) % NX, c, yl, z)


def shift_y(k):
    def move(yh, x, c, yl, z):
        y = (yh * 2 + yl + k) % NY
        return y // 2, x, c, y % 2, z

    return move


def shift_z(k):
    return lambda yh, x, c, yl, z: (yh, x, c, yl, (z + k) % NZ)


def other_core(yh, x, c, yl, z):
    return yh, x, c ^ 1, yl, z


def other_z(yh, x, c, yl, z):
    return yh, x, c, yl, z ^ 1


def other_y_hi(yh, x, c, yl, z):
    return yh ^ 1, x, c, yl, z


def vmem():
    return pl.BlockSpec(memory_space=pltpu.VMEM)


def smem():
    return pl.BlockSpec(memory_space=pltpu.SMEM)


def near(shape, dtype=BF16):
    return pltpu.VMEM(shape, dtype)


def held(value):
    return pltpu.with_memory_space_constraint(value, pltpu.VMEM)


def in_far_memory(value):
    return pltpu.with_memory_space_constraint(value, pltpu.HBM)


def call(kernel, arrays, outs, scratch=(), flops=0, moved=0, limit=12):
    return pl.pallas_call(
        kernel,
        out_shape=outs,
        in_specs=[vmem()] * len(arrays),
        out_specs=[vmem()] * len(outs),
        scratch_shapes=list(scratch),
        compiler_params=pltpu.CompilerParams(vmem_limit_bytes=limit * 1024 * 1024),
        cost_estimate=pl.CostEstimate(flops=flops, bytes_accessed=moved, transcendentals=0),
    )(*arrays)


def place_x():
    return lax.axis_index("x")


def place_y():
    return lax.axis_index("y_hi") * 2 + lax.axis_index("y_lo")


def place_z():
    return lax.axis_index("z_hi") * 2 + lax.axis_index("z_lo")


def halves_kernel(hid, own, other):
    c = lax.axis_index("core")
    low = lax.broadcasted_iota(jnp.int32, (hid.shape[0], CHUNK), 1) < 64
    for x in range(NX):
        first = hid[:, x * CHUNK : (x + 1) * CHUNK].astype(F32)
        second = hid[:, HALF + x * CHUNK : HALF + (x + 1) * CHUNK].astype(F32)
        core0 = jnp.where(low, first, pltpu.roll(second, 64, 1)).astype(BF16)
        core1 = jnp.where(low, pltpu.roll(first, 64, 1), second).astype(BF16)
        cols = slice(x * CHUNK, (x + 1) * CHUNK)
        own[:, cols] = jnp.where(c == 0, core0, core1)
        other[:, cols] = jnp.where(c == 0, core1, core0)


def grad_kernel(offsets, own, other, with_start, *refs):
    refs = list(refs)

    def take(n):
        out, refs[:n] = refs[:n], []
        return out

    n = len(offsets)
    n_src = own + other
    routes = [take(2) for _ in range(n_src)]
    starts = take(2 * n) if with_start else []
    rows = [take(2) for _ in range(n_src)]
    outs = take(4 if offsets == (2,) and with_start else 2 * n)
    acc_a, acc_b = take(2)
    x, y = place_x(), place_y()

    row_loads = []
    if own:
        og, sems = take(2)
        y_first = lax.rem(y + offsets[0], NY)
        for j in range(NY):
            cols = pl.ds(pl.multiple_of(lax.rem(y_first + j, NY) * QUARTER, 128), QUARTER)
            load = pltpu.make_async_copy(rows[0][1].at[:, cols], og.at[:, cols], sems.at[j])
            load.start()
            row_loads.append(load)
        rows[0][1] = og

    def wait_rows(count):
        for load in row_loads[:count]:
            load.wait()
        del row_loads[:count]

    def pairs(expert, add):
        for (listed, counts), (hid, og) in zip(routes, rows):
            count = counts[0, 0, expert]

            def pair_of_tiles(pair, carry):
                t0 = listed[0, 0, expert, 2 * pair]
                t1 = listed[0, 0, expert, 2 * pair + 1]
                r0 = pl.ds(pl.multiple_of(t0 * TILE, TILE), TILE)
                r1 = pl.ds(pl.multiple_of(t1 * TILE, TILE), TILE)
                both = 2 * pair + 1 < count

                def left(at):
                    h1 = hid[r1, at]
                    h1 = jnp.where(both, h1, jnp.zeros_like(h1))
                    return jnp.concatenate([hid[r0, at], h1], axis=0).T

                def right(cols):
                    return jnp.concatenate([og[r0, cols], og[r1, cols]], axis=0)

                add(left, right)
                return carry

            lax.fori_loop(0, (count + 1) // 2, pair_of_tiles, 0)

    def quarter_at(place):
        return pl.ds(pl.multiple_of(place * QUARTER, 128), QUARTER)

    b_outs, a_outs = outs[len(outs) // 2 :], outs[: len(outs) // 2]
    wait_rows(1)
    for i, k in enumerate(offsets):
        if i == 1:
            wait_rows(NY)
        features = quarter_at(lax.rem(y + k, NY))
        if with_start:
            acc_b[...] = starts[n + i][...].astype(F32)
        else:
            acc_b[...] = jnp.zeros_like(acc_b)

        def add_b(left, right):
            values = right(features)

            def half(h, carry):
                at = pl.ds(pl.multiple_of(h * 256, 256), 256)
                acc_b[at, :] += jnp.dot(left(at), values, preferred_element_type=F32)
                return carry

            lax.fori_loop(0, HALF // 256, half, 0)

        pairs(1, add_b)
        if len(outs) > 2 * n:
            b_outs[0][...] = acc_b[: HALF // 2].astype(BF16)
            b_outs[1][...] = acc_b[HALF // 2 :].astype(BF16)
        else:
            b_outs[i][...] = acc_b[...].astype(BF16)
    wait_rows(NY)
    if with_start:
        for i in range(n):
            acc_a[i * CHUNK : (i + 1) * CHUNK] = starts[i][...].astype(F32)
    else:
        acc_a[...] = jnp.zeros_like(acc_a)
    lanes = [
        pl.ds(pl.multiple_of(lax.rem(x + k, NX) * CHUNK, CHUNK), CHUNK) for k in offsets
    ]

    def add_a(left, right):
        turned = [left(at) for at in lanes]
        turned = turned[0] if n == 1 else jnp.concatenate(turned, axis=0)

        def quarter(q, carry):
            cols = quarter_at(q)
            acc_a[:, cols] += jnp.dot(turned, right(cols), preferred_element_type=F32)
            return carry

        lax.fori_loop(0, NY, quarter, 0)

    pairs(0, add_a)
    if len(outs) > 2 * n:
        a_outs[0][...] = acc_a[: CHUNK // 2].astype(BF16)
        a_outs[1][...] = acc_a[CHUNK // 2 :].astype(BF16)
    else:
        for i in range(n):
            a_outs[i][...] = acc_a[i * CHUNK : (i + 1) * CHUNK].astype(BF16)


SHAPE_A, SHAPE_B = (CHUNK, FEATURES), (HALF, QUARTER)


def gradients(offsets, own=None, other=None, starts=()):
    n = len(offsets)
    if offsets == (2,) and starts:
        outs = [near((CHUNK // 2, FEATURES))] * 2 + [near((HALF // 2, QUARTER))] * 2
    else:
        outs = [near(SHAPE_A)] * n + [near(SHAPE_B)] * n
    sources = [source for source in (own, other) if source]
    scratch = [pltpu.VMEM((n * CHUNK, FEATURES), F32), pltpu.VMEM(SHAPE_B, F32)]
    scalars, rows, specs = [], [], []
    for source in sources:
        scalars += source[:2]
        if source is own:
            rows += [held(source[2]), in_far_memory(source[3])]
            specs += [vmem(), pl.BlockSpec(memory_space=pltpu.HBM)]
            scratch += [pltpu.VMEM(source[3].shape, BF16), pltpu.SemaphoreType.DMA((NY,))]
        else:
            rows += [held(source[2]), held(source[3])]
            specs += [vmem()] * 2
    return pl.pallas_call(
        functools.partial(grad_kernel, offsets, own is not None, other is not None, bool(starts)),
        out_shape=outs,
        in_specs=[smem()] * len(scalars) + [vmem()] * len(starts) + specs,
        out_specs=[vmem()] * len(outs),
        scratch_shapes=scratch,
        compiler_params=pltpu.CompilerParams(vmem_limit_bytes=16 * 1024 * 1024),
        cost_estimate=pl.CostEstimate(
            flops=n * len(sources) * 2 * 768 * CHUNK * FEATURES,
            bytes_accessed=(len(sources) * 6 + n * 4) * 2**20,
            transcendentals=0,
        ),
    )(*scalars, *[held(start) for start in starts], *rows)


def add32(*terms):
    total = terms[0].astype(F32)
    for term in terms[1:]:
        total = total + term.astype(F32)
    return total


def after(value, *others):
    return lax.optimization_barrier((value, *others))[0]


def merge_kernel(*refs):
    for i in range(2):
        left, right, far_lo, far_hi = refs[4 * i : 4 * i + 4]
        left_out, right_out = refs[8 + 2 * i : 10 + 2 * i]
        half = left.shape[0] // 2
        left_out[:half] = add32(left[:half], far_lo[...]).astype(BF16)
        left_out[half:] = left[half:]
        right_out[:half] = right[:half]
        right_out[half:] = add32(right[half:], far_hi[...]).astype(BF16)


def cut_kernel(which, own, left, right, *outs):
    for k in range(4):
        if which == 0:
            yk = lax.rem(place_y() + k, NY)
            rows, cols = slice(None), pl.ds(pl.multiple_of(yk * QUARTER, 128), QUARTER)
        else:
            xk = lax.rem(place_x() + k, NX)
            rows, cols = pl.ds(pl.multiple_of(xk * CHUNK, CHUNK), CHUNK), slice(None)
        outs[k][...] = add32(own[rows, cols], left[rows, cols], right[rows, cols]).astype(BF16)


def plane_kernel(*refs):
    keep, give = refs[8:]
    sums = []
    for expert in range(BUCKETS):
        terms = refs[4 * expert : 4 * expert + 4]
        sums.append(add32(*[term[...] for term in terms]))
    even = lax.axis_index("z_lo") == 0
    keep[...] = jnp.where(even, sums[0], sums[1]).astype(BF16)
    give[...] = jnp.where(even, sums[1], sums[0]).astype(BF16)


def pair_kernel(keep, given, *outs):
    for k in range(4):
        group = lax.rem(lax.axis_index("z_hi") + k, 4)
        rows = pl.ds(pl.multiple_of(group * 32, 32), 32)
        outs[k][...] = add32(keep[rows, :], given[rows, :]).astype(BF16)


def acts_kernel(acts, own, other):
    z0 = lax.axis_index("z_lo")
    low = lax.broadcasted_iota(jnp.int32, (64, CHUNK), 1) < 64
    for out, expert in ((own, z0), (other, 1 - z0)):
        for x in range(NX):
            first = acts[expert, :, x * CHUNK : (x + 1) * CHUNK].astype(F32)
            second = acts[expert, :, HALF + x * CHUNK : HALF + (x + 1) * CHUNK].astype(F32)
            core0 = jnp.where(low, first, pltpu.roll(second, 64, 1)).astype(BF16)
            core1 = jnp.where(low, pltpu.roll(first, 64, 1), second).astype(BF16)
            out[:, x * CHUNK : (x + 1) * CHUNK] = core0
            out[:, HALF + x * CHUNK : HALF + (x + 1) * CHUNK] = core1


def base_kernel(momentum, weight, own, other):
    yh, yl, z0 = lax.axis_index("y_hi"), lax.axis_index("y_lo"), lax.axis_index("z_lo")
    for out, which in ((own, yh), (other, 1 - yh)):
        cols = pl.ds(pl.multiple_of((which * 2 + yl) * QUARTER, 128), QUARTER)
        decayed = momentum_decay * momentum[z0, :, cols]
        out[...] = weight[z0, :, cols].astype(F32) - learning_rate * decayed


def weight_kernel(base_o, base_t, own, back2, back4, back6, out, share):
    yh, group = lax.axis_index("y_hi"), lax.axis_index("z_hi")
    for k, grad in enumerate((own, back2, back4, back6)):
        at = lax.rem(group - k + 4, 4)
        rows = pl.ds(pl.multiple_of(at * 32, 32), 32)
        source = pl.ds(pl.multiple_of(lax.rem(at, 2) * 32, 32), 32)
        base = jnp.where(at // 2 == yh, base_o[source, :], base_t[source, :])
        share[rows, :] = grad[...]
        out[rows, :] = (base - learning_rate * grad[...].astype(F32)).astype(BF16)


def product_kernel(share, *refs):
    acts, weights, (slots, left, right) = refs[:4], refs[4:12], refs[12:]
    z0, c, x, y = lax.axis_index("z_lo"), lax.axis_index("core"), place_x(), place_y()
    for i in range(8):
        dc, k = i // 4, i % 4
        group = (c ^ dc) * NX + lax.rem(x - k + NX, NX)
        cols = pl.ds(pl.multiple_of(group * CHUNK, CHUNK), CHUNK)
        at = slice(i * CHUNK, (i + 1) * CHUNK)
        right[at, :] = weights[i][...]
        for j in range(NY):
            for dz in range(2):
                first = dz * 256 + j * 64
                left[first : first + 64, at] = acts[j][dz, :, cols]
    for dz in range(2):
        total = jnp.dot(
            left[dz * 256 : (dz + 1) * 256, :], right[...], preferred_element_type=F32
        ).astype(BF16)
        for j in range(NY):
            y_to = lax.rem(y - j + NY, NY)
            slot = y_to * 2 + (z0 ^ dz)
            slots[slot, 0:64, :] = total[j * 64 : (j + 1) * 64]
            rows = pl.ds(pl.multiple_of((y_to // 2) * 64, 64), 64)
            slots[slot, 64:128, :] = share[rows, :]


def join_kernel(momentum, slots, new_momentum, next_out):
    for slot in range(8):
        quarter, e = slot // 2, slot % 2
        cols = slice(quarter * QUARTER, (quarter + 1) * QUARTER)
        next_out[e, :, cols] = slots[slot, 0:64, :]
        new_momentum[e, :, cols] = momentum_decay * momentum[e, :, cols] + slots[
            slot, 64:128, :
        ].astype(F32)


def local(hidden_act, out_grad, tile_list, tile_count, momentum, weight, next_act):
    rows = hidden_act.shape[0]

    og_t = send(out_grad, other_core)
    hid_o, hid_x = call(
        halves_kernel, [hidden_act], [near((rows, HALF))] * 2, moved=4 * 2**20, limit=16
    )
    hid_t = send(hid_x, other_core)
    own = (tile_list, tile_count, hid_o, out_grad)
    other = (send(tile_list, other_core), send(tile_count, other_core), hid_t, og_t)
    starts = gradients((2,), own)

    acts, acts_x = call(
        acts_kernel, [next_act], [jax.ShapeDtypeStruct((64, 1024), BF16)] * 2, moved=2**20
    )
    acts_z = send(acts_x, other_z)
    base_o, base_x = call(
        base_kernel, [momentum, weight], [near((64, QUARTER), F32)] * 2, moved=4 * 2**20
    )

    lower_a, upper_a, lower_b, upper_b = gradients((2,), None, other, starts)
    far_b = send(lower_b, shift_y(1)), send(upper_b, shift_y(-1))
    far_a = send(lower_a, shift_x(1)), send(upper_a, shift_x(-1))
    left_a, right_a, left_b, right_b = gradients((1, 3), own, other)
    own_a, own_b = gradients((0,), own, other)
    left_a, right_a, left_b, right_b = call(
        merge_kernel,
        [held(v) for v in (left_a, right_a)]
        + list(far_a)
        + [held(v) for v in (left_b, right_b)]
        + list(far_b),
        [near(SHAPE_A)] * 2 + [near(SHAPE_B)] * 2,
        moved=10 * 2**20,
    )

    def cuts(which, own_part, left, right, shift):
        return call(
            functools.partial(cut_kernel, which),
            [held(own_part), send(left, shift(1)), send(right, shift(-1))],
            [near((CHUNK, QUARTER))] * 4,
            moved=4 * 2**20,
        )

    cut_a = cuts(0, own_a, left_a, right_a, shift_x)
    cut_b = cuts(1, own_b, left_b, right_b, shift_y)
    cut_a, cut_b = lax.optimization_barrier((cut_a, cut_b))

    plane_a, plane_b = [cut_a[0]], [cut_b[0]]
    for k in (1, 3, 2):
        plane_a.append(send(cut_a[k], shift_y(k)))
        plane_b.append(send(cut_b[k], shift_x(k)))
    keep, give = call(
        plane_kernel, plane_a + plane_b, [near((CHUNK, QUARTER))] * 2, moved=3 * 2**20
    )
    given = send(give, other_z)
    pair = jnp.stack([acts, acts_z])
    pair = after(pair, give)
    acts_y = [pair] + [send(pair, shift_y(k)) for k in (1, 2, 3)]
    base_t = send(after(base_x, give), other_y_hi)
    groups = call(pair_kernel, [held(keep), given], [near((32, QUARTER))] * 4, moved=2**20)
    grad = add32(groups[0], *[send(groups[k], shift_z(2 * k)) for k in (2, 1, 3)]).astype(BF16)
    back = {k: send(grad, shift_z(k)) for k in (4, 2, 6)}
    own_weight, share = call(
        weight_kernel,
        [held(base_o), base_t, grad] + [back[k] for k in (2, 4, 6)],
        [near((CHUNK, QUARTER))] * 2,
        moved=2**20,
    )
    weights = [own_weight] + [send(own_weight, shift_x(k)) for k in (1, 2, 3)]
    weights += [send(part, other_core) for part in weights]
    (slots,) = call(
        product_kernel,
        [held(share)] + acts_y + weights,
        [jax.ShapeDtypeStruct((8, 128, QUARTER), BF16)],
        [pltpu.VMEM((512, 1024), BF16), pltpu.VMEM((1024, QUARTER), BF16)],
        flops=2 * 512 * 1024 * QUARTER,
        moved=4 * 2**20,
    )
    slots = lax.all_to_all(slots, GROUP, 0, 0)
    new_momentum, next_out = call(
        join_kernel,
        [momentum, slots],
        [
            jax.ShapeDtypeStruct((BUCKETS, 64, FEATURES), F32),
            jax.ShapeDtypeStruct((BUCKETS, 64, FEATURES), BF16),
        ],
        moved=6 * 2**20,
    )
    return new_momentum, next_out


def solution(mesh):
    fine = jax.sharding.Mesh(mesh.devices.reshape(2, NX, 2, 2, NZ // 2, 2), AXES)
    node, replica = AXES[:3], AXES[3:]
    in_specs = (
        P(node + replica, None),
        P(node + replica, None),
        P(node, replica, None, None),
        P(node, replica, None),
        P(None, node, None),
        P(None, node, None),
        P(None, node + replica, None),
    )
    out_specs = (P(None, node, None), P(None, node + replica, None))
    return jax.shard_map(local, mesh=fine, in_specs=in_specs, out_specs=out_specs, check_vma=False)
```

time: 550 us -> 159 us (0.29)
  waiting for transfers between devices: 451 us -> 25.4 us
  starting transfers between devices: 0.39 us -> 62.9 us
  Pallas kernels: 0 us -> 40.4 us
  local copies, waits for them, and re-layouts: 40 us -> 2.75 us
  matrix products: 30.7 us -> 0 us
  blocking collectives: 0 us -> 25.9 us
  other arithmetic: 13 us -> 0.06 us
  between operations: 13.8 us -> 0.88 us
    unnamed x7 -> x0, waiting for transfers between devices: 183 us -> none
    all_gather x2 -> x0, waiting for transfers between devices: 136 us -> none  [local(): lax.all_gather(new_weight, 'node', axis=0, tiled=True)]
    psum x1 -> x0, waiting for transfers between devices: 132 us -> none  [local(): grad_share = lax.psum(node_share, 'replica').astype(jnp.float32)]
    ppermute x0 -> x37, starting transfers between devices: none -> 62.9 us  [send(): return lax.ppermute(value, AXES, pairs)]
    pallas_call x0 -> x15, Pallas kernels: none -> 40.4 us  [the longest x4 34.6 us: gradients(): pl.pallas_call(functools.partial(grad_kernel, offsets, own is not None, o...]
    unnamed x21 -> x12, local copies, waits for them, and re-layouts: 34.2 us -> 2.75 us
    dot_general x4 -> x0, matrix products: 30.7 us -> none  [the longest x2 21.7 us: partial_rows(): lax.dot_general(hidden_act, masked, (((0,), (0,)), ((), ())), preferred_e...]
    all_to_all x0 -> x1, blocking collectives: none -> 25.9 us  [local(): slots = lax.all_to_all(slots, GROUP, 0, 0)]
  transfers between devices with their start and end apart: 5 -> 37, of which waited for: 5 -> 11; matrix products, arithmetic and copies ran while one was open for 8% -> 0% of each run, Pallas kernels for 0% -> 20%
where the time goes in v1:
time: 159 us; the launch traced here: 158 us
  starting transfers between devices  62.9 us (40%)
  Pallas kernels  40.4 us (25%)
  blocking collectives  25.9 us (16%)
  waiting for transfers between devices  25.4 us (16%)
  local copies, waits for them, and re-layouts  2.75 us (2%)
    ppermute x37, starting transfers between devices, send(): return lax.ppermute(value, AXES, pairs)  62.9 us
    pallas_call x4, Pallas kernels, gradients(): pl.pallas_call(functools.partial(grad_kernel, offsets, own is not None, o...  34.6 us
    all_to_all x1, blocking collectives, local(): slots = lax.all_to_all(slots, GROUP, 0, 0)  25.9 us
    ppermute x37, waiting for transfers between devices, send(): return lax.ppermute(value, AXES, pairs)  25.4 us
    pallas_call x11, Pallas kernels, call(): pl.pallas_call(kernel, out_shape=outs, in_specs=[vmem()] * len(arrays), o...  5.8 us
  transfers between devices with their start and end apart: 37, of which 11 were waited for; matrix products, arithmetic and copies ran while one was open for 0% of the time, Pallas kernels for 20%

profile of v1, /device:TPU:1, one launch (start us, length us, event | category | flops | bytes accessed | tf_op | source)
XLA Modules:
  0.0 158.3 jit_solution(16166253569056658618)
XLA Ops:
  0.6 3.3 %collective-permute-start.3 = (bf16[768,3584]{1,0:T(8,128)(2,1)}, bf16[768,3584]{1,0:T(8,128)(2,1)S(1)}, u32[]{:S(2)}, u32[]{:S(2)}) collective-permute-start(bf16[768,3584]{1,0:T(8,128)(2,1)} %refs_3_.1), channel_id=1, source_target_pairs={{0,16},{1,17},{2,18},{3,19},{4,20},{5,21},{6,22},{7,23},{8,24},{9,... | collective-permute-start | bytes 16515080 | tf_op jit(solution)/shard_map/ppermute | solution.py:41
  8.2 6.5 %shard_map.90 = (bf16[128,3584]{1,0:T(8,128)(2,1)S(1)}, bf16[512,896]{1,0:T(8,128)(2,1)S(1)}) custom-call(s32[1,1,2,6]{3,2,1,0:T(2,128)S(1)} %copy-done.4, s32[1,1,2]{2,1,0:T(1,128)S(1)} %copy-done.5, bf16[768,512]{1,0:T(8,128)(2,1)S(1)} %get-tuple-element.52.refs_4_.refs_2_, bf16[768,3584]{1,0:T(8,128)(2,1)} %refs_3_.1), custom_call_target="tpu_custom_call" | custom-call | flops 704643072 | bytes 10485760 | tf_op jit(solution)/shard_map/pallas_call | solution.py:266
  14.7 4.7 %shard_map.91 = (bf16[64,3584]{1,0:T(8,128)(2,1)S(1)}, bf16[64,3584]{1,0:T(8,128)(2,1)S(1)}, bf16[256,896]{1,0:T(8,128)(2,1)S(1)}, bf16[256,896]{1,0:T(8,128)(2,1)S(1)}) custom-call(s32[1,1,2,6]{3,2,1,0:T(2,128)S(1)} %collective-permute-done.refs_2_.refs_0_, s32[1,1,2]{2,1,0:T(1,128)S(1)} %collective-permute-done.1.refs_3_.refs_1_, ...), custom_call_target="tpu_custom_call" | custom-call | flops 704643072 | bytes 10485760 | tf_op jit(solution)/shard_map/pallas_call | solution.py:266
  19.5 2.7 %collective-permute-start.5 = (bf16[64,3584]{1,0:T(8,128)(2,1)S(1)}, bf16[64,3584]{1,0:T(8,128)(2,1)S(1)}, u32[]{:S(2)}, u32[]{:S(2)}) collective-permute-start(bf16[64,3584]{1,0:T(8,128)(2,1)S(1)} %get-tuple-element.60), channel_id=1, source_target_pairs={{0,96},{1,97},{2,98},{3,99},{4,100},{5,101},{6,102},{7,103},{8,104... | collective-permute-start | bytes 1376264 | tf_op jit(solution)/shard_map/ppermute | solution.py:41
  22.2 2.7 %collective-permute-start.7 = (bf16[256,896]{1,0:T(8,128)(2,1)S(1)}, bf16[256,896]{1,0:T(8,128)(2,1)S(1)}, u32[]{:S(2)}, u32[]{:S(2)}) collective-permute-start(bf16[256,896]{1,0:T(8,128)(2,1)S(1)} %get-tuple-element.64), channel_id=1, source_target_pairs={{0,136},{1,137},{2,138},{3,139},{4,140},{5,141},{6,142},{7,143},{8... | collective-permute-start | bytes 1376264 | tf_op jit(solution)/shard_map/ppermute | solution.py:41
  24.9 13.5 %shard_map.89 = (bf16[128,3584]{1,0:T(8,128)(2,1)S(1)}, bf16[128,3584]{1,0:T(8,128)(2,1)S(1)}, bf16[512,896]{1,0:T(8,128)(2,1)S(1)}, bf16[512,896]{1,0:T(8,128)(2,1)S(1)}) custom-call(s32[1,1,2,6]{3,2,1,0:T(2,128)S(1)} %copy-done.4, s32[1,1,2]{2,1,0:T(1,128)S(1)} %copy-done.5, s32[1,1,2,6]{3,2,1,0:T(2,128)S(1)} %collective-permute-done.refs_2_.refs_0_, ...), custom_call_target="tpu_custom_call" | custom-call | flops 2818572288 | bytes 20971520 | tf_op jit(solution)/shard_map/pallas_call | solution.py:266
  39.0 2.7 %collective-permute-start.9 = (bf16[128,3584]{1,0:T(8,128)(2,1)S(1)}, bf16[128,3584]{1,0:T(8,128)(2,1)S(1)}, u32[]{:S(2)}, u32[]{:S(2)}) collective-permute-start(bf16[128,3584]{1,0:T(8,128)(2,1)S(1)} %get-tuple-element.66), channel_id=1, source_target_pairs={{0,96},{1,97},{2,98},{3,99},{4,100},{5,101},{6,102},{7,103},{8,104... | collective-permute-start | bytes 2752520 | tf_op jit(solution)/shard_map/ppermute | solution.py:41
  41.7 2.7 %collective-permute-start.11 = (bf16[512,896]{1,0:T(8,128)(2,1)S(1)}, bf16[512,896]{1,0:T(8,128)(2,1)S(1)}, u32[]{:S(2)}, u32[]{:S(2)}) collective-permute-start(bf16[512,896]{1,0:T(8,128)(2,1)S(1)} %get-tuple-element.73), channel_id=1, source_target_pairs={{0,136},{1,137},{2,138},{3,139},{4,140},{5,141},{6,142},{7,143},{8... | collective-permute-start | bytes 2752520 | tf_op jit(solution)/shard_map/ppermute | solution.py:41
  44.3 9.9 %shard_map.88 = (bf16[128,3584]{1,0:T(8,128)(2,1)S(1)}, bf16[512,896]{1,0:T(8,128)(2,1)S(1)}) custom-call(s32[1,1,2,6]{3,2,1,0:T(2,128)S(1)} %copy-done.4, s32[1,1,2]{2,1,0:T(1,128)S(1)} %copy-done.5, s32[1,1,2,6]{3,2,1,0:T(2,128)S(1)} %collective-permute-done.refs_2_.refs_0_, s32[1,1,2]{2,1,0:T(1,128)S(1)} %collective-permute-done.1.refs_3_.refs_1_, ...), custom_call_target="tpu_custom_call" | custom-call | flops 1409286144 | bytes 16777216 | tf_op jit(solution)/shard_map/pallas_call | solution.py:266
  54.3 6.2 %collective-permute-done.8.left = bf16[128,3584]{1,0:T(8,128)(2,1)S(1)} collective-permute-done((bf16[128,3584]{1,0:T(8,128)(2,1)S(1)}, bf16[128,3584]{1,0:T(8,128)(2,1)S(1)}, u32[]{:S(2)}, u32[]{:S(2)}) %collective-permute-start.8) | collective-permute-done | bytes 917536 | tf_op jit(solution)/shard_map/ppermute | solution.py:41
  63.1 2.7 %collective-permute-start.13 = (bf16[128,896]{1,0:T(8,128)(2,1)S(1)}, bf16[128,896]{1,0:T(8,128)(2,1)S(1)}, u32[]{:S(2)}, u32[]{:S(2)}) collective-permute-start(bf16[128,896]{1,0:T(8,128)(2,1)S(1)} %get-tuple-element.80), channel_id=1, source_target_pairs={{0,136},{1,137},{2,138},{3,139},{4,140},{5,141},{6,142},{7,143},{8... | collective-permute-start | bytes 688136 | tf_op jit(solution)/shard_map/ppermute | solution.py:41
  66.6 2.7 %collective-permute-start.16 = (bf16[128,896]{1,0:T(8,128)(2,1)S(1)}, bf16[128,896]{1,0:T(8,128)(2,1)S(1)}, u32[]{:S(2)}, u32[]{:S(2)}) collective-permute-start(bf16[128,896]{1,0:T(8,128)(2,1)S(1)} %get-tuple-element.84), channel_id=1, source_target_pairs={{0,96},{1,97},{2,98},{3,99},{4,100},{5,101},{6,102},{7,103},{8,104... | collective-permute-start | bytes 688136 | tf_op jit(solution)/shard_map/ppermute | solution.py:41
  70.1 3.4 %collective-permute-done.14.refs_3_ = bf16[128,896]{1,0:T(8,128)(2,1)S(1)} collective-permute-done((bf16[128,896]{1,0:T(8,128)(2,1)S(1)}, bf16[128,896]{1,0:T(8,128)(2,1)S(1)}, u32[]{:S(2)}, u32[]{:S(2)}) %collective-permute-start.14) | collective-permute-done | bytes 229408 | tf_op jit(solution)/shard_map/ppermute | solution.py:41
  74.8 3.3 %collective-permute-done.17.refs_7_ = bf16[128,896]{1,0:T(8,128)(2,1)S(1)} collective-permute-done((bf16[128,896]{1,0:T(8,128)(2,1)S(1)}, bf16[128,896]{1,0:T(8,128)(2,1)S(1)}, u32[]{:S(2)}, u32[]{:S(2)}) %collective-permute-start.17) | collective-permute-done | bytes 229408 | tf_op jit(solution)/shard_map/ppermute | solution.py:41
  80.2 3.1 %collective-permute-done.19.given = bf16[128,896]{1,0:T(8,128)(2,1)S(1)} collective-permute-done((bf16[128,896]{1,0:T(8,128)(2,1)S(1)}, bf16[128,896]{1,0:T(8,128)(2,1)S(1)}, u32[]{:S(2)}, u32[]{:S(2)}) %collective-permute-start.19) | collective-permute-done | bytes 229408 | tf_op jit(solution)/shard_map/ppermute | solution.py:41
  83.4 4.4 %collective-permute-start.20 = (bf16[32,896]{1,0:T(8,128)(2,1)S(1)}, bf16[32,896]{1,0:T(8,128)(2,1)S(1)}, u32[]{:S(2)}, u32[]{:S(2)}) collective-permute-start(bf16[32,896]{1,0:T(8,128)(2,1)S(1)} %get-tuple-element.90), channel_id=1, source_target_pairs={{0,4},{1,5},{2,6},{3,7},{4,0},{5,1},{6,2},{7,3},{8,12},{9,13},{10,... | collective-permute-start | bytes 172040 | tf_op jit(solution)/shard_map/ppermute | solution.py:41
  91.4 2.8 %collective-permute-start.18 = (f32[64,896]{1,0:T(8,128)S(1)}, f32[64,896]{1,0:T(8,128)S(1)}, u32[]{:S(2)}, u32[]{:S(2)}) collective-permute-start(f32[64,896]{1,0:T(8,128)S(1)} %get-tuple-element.87), channel_id=1, source_target_pairs={{0,128},{1,129},{2,130},{3,131},{4,132},{5,133},{6,134},{7,135},{8... | collective-permute-start | bytes 688136 | tf_op jit(solution)/shard_map/ppermute | solution.py:41
  99.1 2.5 %collective-permute-start.28 = (bf16[2,64,1024]{2,1,0:T(8,128)(2,1)S(1)}, bf16[2,64,1024]{2,1,0:T(8,128)(2,1)S(1)}, u32[]{:S(2)}, u32[]{:S(2)}) collective-permute-start(bf16[2,64,1024]{2,1,0:T(8,128)(2,1)S(1)} %pad_maximum_fusion.refs_0_), channel_id=1, source_target_pairs={{0,128},{1,129},{2,130},{3,131},{4,132},{5,133},{6,134},{7,135},{8... | collective-permute-start | bytes 786440 | tf_op jit(solution)/shard_map/ppermute | solution.py:41
  101.6 2.4 %collective-permute-done.24.back4 = bf16[32,896]{1,0:T(8,128)(2,1)S(1)} collective-permute-done((bf16[32,896]{1,0:T(8,128)(2,1)S(1)}, bf16[32,896]{1,0:T(8,128)(2,1)S(1)}, u32[]{:S(2)}, u32[]{:S(2)}) %collective-permute-start.24) | collective-permute-done | bytes 57376 | tf_op jit(solution)/shard_map/ppermute | solution.py:41
  108.3 11.6 %collective-permute-start.33 = (bf16[128,896]{1,0:T(8,128)(2,1)S(1)}, bf16[128,896]{1,0:T(8,128)(2,1)S(1)}, u32[]{:S(2)}, u32[]{:S(2)}) collective-permute-start(bf16[128,896]{1,0:T(8,128)(2,1)S(1)} %get-tuple-element.97.refs_4_), channel_id=1, source_target_pairs={{0,16},{1,17},{2,18},{3,19},{4,20},{5,21},{6,22},{7,23},{8,24},{9,... | collective-permute-start | bytes 688136 | tf_op jit(solution)/shard_map/ppermute | solution.py:41
  120.0 3.0 %collective-permute-start.36 = (bf16[128,896]{1,0:T(8,128)(2,1)S(1)}, bf16[128,896]{1,0:T(8,128)(2,1)S(1)}, u32[]{:S(2)}, u32[]{:S(2)}) collective-permute-start(bf16[128,896]{1,0:T(8,128)(2,1)S(1)} %collective-permute-done.32.refs_7_), channel_id=1, source_target_pairs={{0,16},{1,17},{2,18},{3,19},{4,20},{5,21},{6,22},{7,23},{8,24},{9,... | collective-permute-start | bytes 688136 | tf_op jit(solution)/shard_map/ppermute | solution.py:41
  122.9 2.8 %collective-permute-start.35 = (bf16[128,896]{1,0:T(8,128)(2,1)S(1)}, bf16[128,896]{1,0:T(8,128)(2,1)S(1)}, u32[]{:S(2)}, u32[]{:S(2)}) collective-permute-start(bf16[128,896]{1,0:T(8,128)(2,1)S(1)} %collective-permute-done.31.refs_6_), channel_id=1, source_target_pairs={{0,16},{1,17},{2,18},{3,19},{4,20},{5,21},{6,22},{7,23},{8,24},{9,... | collective-permute-start | bytes 688136 | tf_op jit(solution)/shard_map/ppermute | solution.py:41
  125.7 2.3 %collective-permute-start.34 = (bf16[128,896]{1,0:T(8,128)(2,1)S(1)}, bf16[128,896]{1,0:T(8,128)(2,1)S(1)}, u32[]{:S(2)}, u32[]{:S(2)}) collective-permute-start(bf16[128,896]{1,0:T(8,128)(2,1)S(1)} %collective-permute-done.30.refs_5_), channel_id=1, source_target_pairs={{0,16},{1,17},{2,18},{3,19},{4,20},{5,21},{6,22},{7,23},{8,24},{9,... | collective-permute-start | bytes 688136 | tf_op jit(solution)/shard_map/ppermute | solution.py:41
  130.6 25.9 %all_to_all.5.slots = bf16[8,128,896]{2,1,0:T(8,128)(2,1)S(1)} all-to-all(bf16[8,128,896]{2,1,0:T(8,128)(2,1)S(1)} %shard_map.99), channel_id=1, replica_groups=mesh['y_hi'=2,'x'=4,'core'=2,'y_lo'=2,'z_hi'=4,'z_lo'=2] {'y_hi','y_lo',..., dimensions={0} | all-to-all | bytes 3670016 | tf_op jit(solution)/shard_map/all_to_all | solution.py:477
  (80 shorter events, 29.8 us)
Async XLA Ops:
  0.6 14.1 %collective-permute-start.3 = (bf16[768,3584]{1,0:T(8,128)(2,1)}, bf16[768,3584]{1,0:T(8,128)(2,1)S(1)}, u32[]{:S(2)}, u32[]{:S(2)}) collective-permute-start(bf16[768,3584]{1,0:T(8,128)(2,1)} %refs_3_.1), channel_id=1, source_target_pairs={{0,16},{1,17},{2,18},{3,19},{4,20},{5,21},{6,22},{7,23},{8,24},{9,... | collective-permute-start | bytes 16515080 | tf_op jit(solution)/shard_map/ppermute | solution.py:41
  6.1 8.5 %collective-permute-start.2 = (bf16[768,512]{1,0:T(8,128)(2,1)S(1)}, bf16[768,512]{1,0:T(8,128)(2,1)S(1)}, u32[]{:S(2)}, u32[]{:S(2)}) collective-permute-start(bf16[768,512]{1,0:T(8,128)(2,1)S(1)} %get-tuple-element.53), channel_id=1, source_target_pairs={{0,16},{1,17},{2,18},{3,19},{4,20},{5,21},{6,22},{7,23},{8,24},{9,... | collective-permute-start | bytes 2359304 | tf_op jit(solution)/shard_map/ppermute | solution.py:41
  6.3 8.4 %collective-permute-start.1 = (s32[1,1,2]{2,1,0:T(1,128)}, s32[1,1,2]{2,1,0:T(1,128)S(1)}, u32[]{:S(2)}, u32[]{:S(2)}) collective-permute-start(s32[1,1,2]{2,1,0:T(1,128)} %refs_1_.5), channel_id=1, source_target_pairs={{0,16},{1,17},{2,18},{3,19},{4,20},{5,21},{6,22},{7,23},{8,24},{9,... | collective-permute-start | bytes 32 | tf_op jit(solution)/shard_map/ppermute | solution.py:41
  6.7 7.9 %collective-permute-start = (s32[1,1,2,6]{3,2,1,0:T(2,128)}, s32[1,1,2,6]{3,2,1,0:T(2,128)S(1)}, u32[]{:S(2)}, u32[]{:S(2)}) collective-permute-start(s32[1,1,2,6]{3,2,1,0:T(2,128)} %refs_0_.5), channel_id=1, source_target_pairs={{0,16},{1,17},{2,18},{3,19},{4,20},{5,21},{6,22},{7,23},{8,24},{9,... | collective-permute-start | bytes 152 | tf_op jit(solution)/shard_map/ppermute | solution.py:41
  19.5 18.9 %collective-permute-start.4 = (bf16[64,3584]{1,0:T(8,128)(2,1)S(1)}, bf16[64,3584]{1,0:T(8,128)(2,1)S(1)}, u32[]{:S(2)}, u32[]{:S(2)}) collective-permute-start(bf16[64,3584]{1,0:T(8,128)(2,1)S(1)} %get-tuple-element.59), channel_id=1, source_target_pairs={{0,32},{1,33},{2,34},{3,35},{4,36},{5,37},{6,38},{7,39},{8,40},{9,... | collective-permute-start | bytes 1376264 | tf_op jit(solution)/shard_map/ppermute | solution.py:41
  19.5 18.8 %collective-permute-start.5 = (bf16[64,3584]{1,0:T(8,128)(2,1)S(1)}, bf16[64,3584]{1,0:T(8,128)(2,1)S(1)}, u32[]{:S(2)}, u32[]{:S(2)}) collective-permute-start(bf16[64,3584]{1,0:T(8,128)(2,1)S(1)} %get-tuple-element.60), channel_id=1, source_target_pairs={{0,96},{1,97},{2,98},{3,99},{4,100},{5,101},{6,102},{7,103},{8,104... | collective-permute-start | bytes 1376264 | tf_op jit(solution)/shard_map/ppermute | solution.py:41
  22.2 16.2 %collective-permute-start.6 = (bf16[256,896]{1,0:T(8,128)(2,1)S(1)}, bf16[256,896]{1,0:T(8,128)(2,1)S(1)}, u32[]{:S(2)}, u32[]{:S(2)}) collective-permute-start(bf16[256,896]{1,0:T(8,128)(2,1)S(1)} %get-tuple-element.63), channel_id=1, source_target_pairs={{0,8},{1,9},{2,10},{3,11},{4,12},{5,13},{6,14},{7,15},{8,128},{9,1... | collective-permute-start | bytes 1376264 | tf_op jit(solution)/shard_map/ppermute | solution.py:41
  22.2 16.2 %collective-permute-start.7 = (bf16[256,896]{1,0:T(8,128)(2,1)S(1)}, bf16[256,896]{1,0:T(8,128)(2,1)S(1)}, u32[]{:S(2)}, u32[]{:S(2)}) collective-permute-start(bf16[256,896]{1,0:T(8,128)(2,1)S(1)} %get-tuple-element.64), channel_id=1, source_target_pairs={{0,136},{1,137},{2,138},{3,139},{4,140},{5,141},{6,142},{7,143},{8... | collective-permute-start | bytes 1376264 | tf_op jit(solution)/shard_map/ppermute | solution.py:41
  38.9 21.6 %collective-permute-start.8 = (bf16[128,3584]{1,0:T(8,128)(2,1)S(1)}, bf16[128,3584]{1,0:T(8,128)(2,1)S(1)}, u32[]{:S(2)}, u32[]{:S(2)}) collective-permute-start(bf16[128,3584]{1,0:T(8,128)(2,1)S(1)} %get-tuple-element.65), channel_id=1, source_target_pairs={{0,32},{1,33},{2,34},{3,35},{4,36},{5,37},{6,38},{7,39},{8,40},{9,... | collective-permute-start | bytes 2752520 | tf_op jit(solution)/shard_map/ppermute | solution.py:41
  39.0 21.5 %collective-permute-start.9 = (bf16[128,3584]{1,0:T(8,128)(2,1)S(1)}, bf16[128,3584]{1,0:T(8,128)(2,1)S(1)}, u32[]{:S(2)}, u32[]{:S(2)}) collective-permute-start(bf16[128,3584]{1,0:T(8,128)(2,1)S(1)} %get-tuple-element.66), channel_id=1, source_target_pairs={{0,96},{1,97},{2,98},{3,99},{4,100},{5,101},{6,102},{7,103},{8,104... | collective-permute-start | bytes 2752520 | tf_op jit(solution)/shard_map/ppermute | solution.py:41
  41.7 21.0 %collective-permute-start.10 = (bf16[512,896]{1,0:T(8,128)(2,1)S(1)}, bf16[512,896]{1,0:T(8,128)(2,1)S(1)}, u32[]{:S(2)}, u32[]{:S(2)}) collective-permute-start(bf16[512,896]{1,0:T(8,128)(2,1)S(1)} %get-tuple-element.72), channel_id=1, source_target_pairs={{0,8},{1,9},{2,10},{3,11},{4,12},{5,13},{6,14},{7,15},{8,128},{9,1... | collective-permute-start | bytes 2752520 | tf_op jit(solution)/shard_map/ppermute | solution.py:41
  41.7 21.0 %collective-permute-start.11 = (bf16[512,896]{1,0:T(8,128)(2,1)S(1)}, bf16[512,896]{1,0:T(8,128)(2,1)S(1)}, u32[]{:S(2)}, u32[]{:S(2)}) collective-permute-start(bf16[512,896]{1,0:T(8,128)(2,1)S(1)} %get-tuple-element.73), channel_id=1, source_target_pairs={{0,136},{1,137},{2,138},{3,139},{4,140},{5,141},{6,142},{7,143},{8... | collective-permute-start | bytes 2752520 | tf_op jit(solution)/shard_map/ppermute | solution.py:41
  66.6 8.2 %collective-permute-start.16 = (bf16[128,896]{1,0:T(8,128)(2,1)S(1)}, bf16[128,896]{1,0:T(8,128)(2,1)S(1)}, u32[]{:S(2)}, u32[]{:S(2)}) collective-permute-start(bf16[128,896]{1,0:T(8,128)(2,1)S(1)} %get-tuple-element.84), channel_id=1, source_target_pairs={{0,96},{1,97},{2,98},{3,99},{4,100},{5,101},{6,102},{7,103},{8,104... | collective-permute-start | bytes 688136 | tf_op jit(solution)/shard_map/ppermute | solution.py:41
  69.3 8.8 %collective-permute-start.17 = (bf16[128,896]{1,0:T(8,128)(2,1)S(1)}, bf16[128,896]{1,0:T(8,128)(2,1)S(1)}, u32[]{:S(2)}, u32[]{:S(2)}) collective-permute-start(bf16[128,896]{1,0:T(8,128)(2,1)S(1)} %get-tuple-element.85), channel_id=1, source_target_pairs={{0,64},{1,65},{2,66},{3,67},{4,68},{5,69},{6,70},{7,71},{8,72},{9,... | collective-permute-start | bytes 688136 | tf_op jit(solution)/shard_map/ppermute | solution.py:41
  78.6 12.8 %collective-permute-start.26 = (bf16[64,1024]{1,0:T(8,128)(2,1)S(1)}, bf16[64,1024]{1,0:T(8,128)(2,1)S(1)}, u32[]{:S(2)}, u32[]{:S(2)}) collective-permute-start(bf16[64,1024]{1,0:T(8,128)(2,1)S(1)} %get-tuple-element.95), channel_id=1, source_target_pairs={{0,1},{1,0},{2,3},{3,2},{4,5},{5,4},{6,7},{7,6},{8,9},{9,8},{10,11... | collective-permute-start | bytes 393224 | tf_op jit(solution)/shard_map/ppermute | solution.py:41
  83.4 11.5 %collective-permute-start.20 = (bf16[32,896]{1,0:T(8,128)(2,1)S(1)}, bf16[32,896]{1,0:T(8,128)(2,1)S(1)}, u32[]{:S(2)}, u32[]{:S(2)}) collective-permute-start(bf16[32,896]{1,0:T(8,128)(2,1)S(1)} %get-tuple-element.90), channel_id=1, source_target_pairs={{0,4},{1,5},{2,6},{3,7},{4,0},{5,1},{6,2},{7,3},{8,12},{9,13},{10,... | collective-permute-start | bytes 172040 | tf_op jit(solution)/shard_map/ppermute | solution.py:41
  94.2 12.3 %collective-permute-start.29 = (bf16[2,64,1024]{2,1,0:T(8,128)(2,1)S(1)}, bf16[2,64,1024]{2,1,0:T(8,128)(2,1)S(1)}, u32[]{:S(2)}, u32[]{:S(2)}) collective-permute-start(bf16[2,64,1024]{2,1,0:T(8,128)(2,1)S(1)} %pad_maximum_fusion.refs_0_), channel_id=1, source_target_pairs={{0,136},{1,137},{2,138},{3,139},{4,140},{5,141},{6,142},{7,143},{8... | collective-permute-start | bytes 786440 | tf_op jit(solution)/shard_map/ppermute | solution.py:41
  99.1 9.2 %collective-permute-start.28 = (bf16[2,64,1024]{2,1,0:T(8,128)(2,1)S(1)}, bf16[2,64,1024]{2,1,0:T(8,128)(2,1)S(1)}, u32[]{:S(2)}, u32[]{:S(2)}) collective-permute-start(bf16[2,64,1024]{2,1,0:T(8,128)(2,1)S(1)} %pad_maximum_fusion.refs_0_), channel_id=1, source_target_pairs={{0,128},{1,129},{2,130},{3,131},{4,132},{5,133},{6,134},{7,135},{8... | collective-permute-start | bytes 786440 | tf_op jit(solution)/shard_map/ppermute | solution.py:41
  104.9 15.0 %collective-permute-start.32 = (bf16[128,896]{1,0:T(8,128)(2,1)S(1)}, bf16[128,896]{1,0:T(8,128)(2,1)S(1)}, u32[]{:S(2)}, u32[]{:S(2)}) collective-permute-start(bf16[128,896]{1,0:T(8,128)(2,1)S(1)} %get-tuple-element.97.refs_4_), channel_id=1, source_target_pairs={{0,96},{1,97},{2,98},{3,99},{4,100},{5,101},{6,102},{7,103},{8,104... | collective-permute-start | bytes 688136 | tf_op jit(solution)/shard_map/ppermute | solution.py:41
  105.7 17.3 %collective-permute-start.31 = (bf16[128,896]{1,0:T(8,128)(2,1)S(1)}, bf16[128,896]{1,0:T(8,128)(2,1)S(1)}, u32[]{:S(2)}, u32[]{:S(2)}) collective-permute-start(bf16[128,896]{1,0:T(8,128)(2,1)S(1)} %get-tuple-element.97.refs_4_), channel_id=1, source_target_pairs={{0,64},{1,65},{2,66},{3,67},{4,68},{5,69},{6,70},{7,71},{8,72},{9,... | collective-permute-start | bytes 688136 | tf_op jit(solution)/shard_map/ppermute | solution.py:41
  105.9 19.9 %collective-permute-start.30 = (bf16[128,896]{1,0:T(8,128)(2,1)S(1)}, bf16[128,896]{1,0:T(8,128)(2,1)S(1)}, u32[]{:S(2)}, u32[]{:S(2)}) collective-permute-start(bf16[128,896]{1,0:T(8,128)(2,1)S(1)} %get-tuple-element.97.refs_4_), channel_id=1, source_target_pairs={{0,32},{1,33},{2,34},{3,35},{4,36},{5,37},{6,38},{7,39},{8,40},{9,... | collective-permute-start | bytes 688136 | tf_op jit(solution)/shard_map/ppermute | solution.py:41
  106.5 21.6 %collective-permute-start.27 = (bf16[2,64,1024]{2,1,0:T(8,128)(2,1)S(1)}, bf16[2,64,1024]{2,1,0:T(8,128)(2,1)S(1)}, u32[]{:S(2)}, u32[]{:S(2)}) collective-permute-start(bf16[2,64,1024]{2,1,0:T(8,128)(2,1)S(1)} %pad_maximum_fusion.refs_0_), channel_id=1, source_target_pairs={{0,8},{1,9},{2,10},{3,11},{4,12},{5,13},{6,14},{7,15},{8,128},{9,1... | collective-permute-start | bytes 786440 | tf_op jit(solution)/shard_map/ppermute | solution.py:41
  108.3 19.7 %collective-permute-start.33 = (bf16[128,896]{1,0:T(8,128)(2,1)S(1)}, bf16[128,896]{1,0:T(8,128)(2,1)S(1)}, u32[]{:S(2)}, u32[]{:S(2)}) collective-permute-start(bf16[128,896]{1,0:T(8,128)(2,1)S(1)} %get-tuple-element.97.refs_4_), channel_id=1, source_target_pairs={{0,16},{1,17},{2,18},{3,19},{4,20},{5,21},{6,22},{7,23},{8,24},{9,... | collective-permute-start | bytes 688136 | tf_op jit(solution)/shard_map/ppermute | solution.py:41
  120.0 8.1 %collective-permute-start.36 = (bf16[128,896]{1,0:T(8,128)(2,1)S(1)}, bf16[128,896]{1,0:T(8,128)(2,1)S(1)}, u32[]{:S(2)}, u32[]{:S(2)}) collective-permute-start(bf16[128,896]{1,0:T(8,128)(2,1)S(1)} %collective-permute-done.32.refs_7_), channel_id=1, source_target_pairs={{0,16},{1,17},{2,18},{3,19},{4,20},{5,21},{6,22},{7,23},{8,24},{9,... | collective-permute-start | bytes 688136 | tf_op jit(solution)/shard_map/ppermute | solution.py:41
  (19 other events, 135.3 us)

commit v2 on v1

--- a/solution.py
+++ b/solution.py
@@ -65,6 +65,10 @@
     return yh, x, c, yl, z ^ 1
 
 
+def other_y_lo(yh, x, c, yl, z):
+    return yh, x, c, yl ^ 1, z
+
+
 def other_y_hi(yh, x, c, yl, z):
     return yh ^ 1, x, c, yl, z
 
@@ -119,11 +123,11 @@
     for x in range(NX):
         first = hid[:, x * CHUNK : (x + 1) * CHUNK].astype(F32)
         second = hid[:, HALF + x * CHUNK : HALF + (x + 1) * CHUNK].astype(F32)
-        core0 = jnp.where(low, first, pltpu.roll(second, 64, 1)).astype(BF16)
-        core1 = jnp.where(low, pltpu.roll(first, 64, 1), second).astype(BF16)
-        cols = slice(x * CHUNK, (x + 1) * CHUNK)
-        own[:, cols] = jnp.where(c == 0, core0, core1)
-        other[:, cols] = jnp.where(c == 0, core1, core0)
+        core0 = jnp.where(low, first, pltpu.roll(second, 64, 1)).astype(BF16).T
+        core1 = jnp.where(low, pltpu.roll(first, 64, 1), second).astype(BF16).T
+        units = slice(x * CHUNK, (x + 1) * CHUNK)
+        own[units, :] = jnp.where(c == 0, core0, core1)
+        other[units, :] = jnp.where(c == 0, core1, core0)
 
 
 def grad_kernel(offsets, own, other, with_start, *refs):
@@ -139,9 +143,9 @@
     starts = take(2 * n) if with_start else []
     rows = [take(2) for _ in range(n_src)]
     outs = take(4 if offsets == (2,) and with_start else 2 * n)
-    acc_a, acc_b = take(2)
     x, y = place_x(), place_y()
 
+    (halves,) = take(1)
     row_loads = []
     if own:
         og, sems = take(2)
@@ -158,29 +162,16 @@
             load.wait()
         del row_loads[:count]
 
-    def pairs(expert, add):
-        for (listed, counts), (hid, og) in zip(routes, rows):
-            count = counts[0, 0, expert]
-
-            def pair_of_tiles(pair, carry):
-                t0 = listed[0, 0, expert, 2 * pair]
-                t1 = listed[0, 0, expert, 2 * pair + 1]
-                r0 = pl.ds(pl.multiple_of(t0 * TILE, TILE), TILE)
-                r1 = pl.ds(pl.multiple_of(t1 * TILE, TILE), TILE)
-                both = 2 * pair + 1 < count
-
-                def left(at):
-                    h1 = hid[r1, at]
-                    h1 = jnp.where(both, h1, jnp.zeros_like(h1))
-                    return jnp.concatenate([hid[r0, at], h1], axis=0).T
-
-                def right(cols):
-                    return jnp.concatenate([og[r0, cols], og[r1, cols]], axis=0)
-
-                add(left, right)
-                return carry
-
-            lax.fori_loop(0, (count + 1) // 2, pair_of_tiles, 0)
+    def owned(route, expert):
+        listed, counts = route
+        tile = lax.broadcasted_iota(jnp.int32, (1, TILES * TILE), 1) // TILE
+        named = tile < 0
+        for i in range(TILES):
+            at = jnp.where(i < counts[0, 0, expert], listed[0, 0, expert, i], -1)
+            named = jnp.logical_or(named, tile == at)
+        return jnp.where(named, 1.0, 0.0).astype(BF16)
+
+    masks = [[owned(route, expert) for expert in range(BUCKETS)] for route in routes]
 
     def quarter_at(place):
         return pl.ds(pl.multiple_of(place * QUARTER, 128), QUARTER)
@@ -191,55 +182,47 @@
         if i == 1:
             wait_rows(NY)
         features = quarter_at(lax.rem(y + k, NY))
-        if with_start:
-            acc_b[...] = starts[n + i][...].astype(F32)
-        else:
-            acc_b[...] = jnp.zeros_like(acc_b)
-
-        def add_b(left, right):
-            values = right(features)
-
-            def half(h, carry):
-                at = pl.ds(pl.multiple_of(h * 256, 256), 256)
-                acc_b[at, :] += jnp.dot(left(at), values, preferred_element_type=F32)
-                return carry
-
-            lax.fori_loop(0, HALF // 256, half, 0)
-
-        pairs(1, add_b)
+
+        def half(h, carry):
+            at = pl.ds(pl.multiple_of(h * 256, 256), 256)
+            total = starts[n + i][at, :].astype(F32) if with_start else None
+            for mask, (hid, og) in zip(masks, rows):
+                term = jnp.dot(hid[at, :] * mask[1], og[:, features], preferred_element_type=F32)
+                total = term if total is None else total + term
+            if len(outs) > 2 * n:
+                halves[at, :] = total.astype(BF16)
+            else:
+                b_outs[i][at, :] = total.astype(BF16)
+            return carry
+
+        lax.fori_loop(0, HALF // 256, half, 0)
         if len(outs) > 2 * n:
-            b_outs[0][...] = acc_b[: HALF // 2].astype(BF16)
-            b_outs[1][...] = acc_b[HALF // 2 :].astype(BF16)
-        else:
-            b_outs[i][...] = acc_b[...].astype(BF16)
+            b_outs[0][...] = halves[: HALF // 2]
+            b_outs[1][...] = halves[HALF // 2 :]
     wait_rows(NY)
-    if with_start:
-        for i in range(n):
-            acc_a[i * CHUNK : (i + 1) * CHUNK] = starts[i][...].astype(F32)
-    else:
-        acc_a[...] = jnp.zeros_like(acc_a)
-    lanes = [
+    units = [
         pl.ds(pl.multiple_of(lax.rem(x + k, NX) * CHUNK, CHUNK), CHUNK) for k in offsets
     ]
 
-    def add_a(left, right):
-        turned = [left(at) for at in lanes]
-        turned = turned[0] if n == 1 else jnp.concatenate(turned, axis=0)
-
-        def quarter(q, carry):
-            cols = quarter_at(q)
-            acc_a[:, cols] += jnp.dot(turned, right(cols), preferred_element_type=F32)
-            return carry
-
-        lax.fori_loop(0, NY, quarter, 0)
-
-    pairs(0, add_a)
-    if len(outs) > 2 * n:
-        a_outs[0][...] = acc_a[: CHUNK // 2].astype(BF16)
-        a_outs[1][...] = acc_a[CHUNK // 2 :].astype(BF16)
-    else:
-        for i in range(n):
-            a_outs[i][...] = acc_a[i * CHUNK : (i + 1) * CHUNK].astype(BF16)
+    def quarter(q, carry):
+        cols = quarter_at(q)
+        total = None
+        if with_start:
+            total = starts[0][:, cols].astype(F32)
+        for mask, (hid, og) in zip(masks, rows):
+            left = [hid[at, :] * mask[0] for at in units]
+            left = left[0] if n == 1 else jnp.concatenate(left, axis=0)
+            term = jnp.dot(left, og[:, cols], preferred_element_type=F32)
+            total = term if total is None else total + term
+        if len(outs) > 2 * n:
+            a_outs[0][:, cols] = total[: CHUNK // 2].astype(BF16)
+            a_outs[1][:, cols] = total[CHUNK // 2 :].astype(BF16)
+        else:
+            for i in range(n):
+                a_outs[i][:, cols] = total[i * CHUNK : (i + 1) * CHUNK].astype(BF16)
+        return carry
+
+    lax.fori_loop(0, NY, quarter, 0)
 
 
 SHAPE_A, SHAPE_B = (CHUNK, FEATURES), (HALF, QUARTER)
@@ -252,7 +235,7 @@
     else:
         outs = [near(SHAPE_A)] * n + [near(SHAPE_B)] * n
     sources = [source for source in (own, other) if source]
-    scratch = [pltpu.VMEM((n * CHUNK, FEATURES), F32), pltpu.VMEM(SHAPE_B, F32)]
+    scratch = [pltpu.VMEM(SHAPE_B, BF16)]
     scalars, rows, specs = [], [], []
     for source in sources:
         scalars += source[:2]
@@ -322,11 +305,8 @@
     give[...] = jnp.where(even, sums[1], sums[0]).astype(BF16)
 
 
-def pair_kernel(keep, given, *outs):
-    for k in range(4):
-        group = lax.rem(lax.axis_index("z_hi") + k, 4)
-        rows = pl.ds(pl.multiple_of(group * 32, 32), 32)
-        outs[k][...] = add32(keep[rows, :], given[rows, :]).astype(BF16)
+def pair_kernel(keep, given, out):
+    out[...] = add32(keep[...], given[...]).astype(BF16)
 
 
 def acts_kernel(acts, own, other):
@@ -350,19 +330,20 @@
         out[...] = weight[z0, :, cols].astype(F32) - learning_rate * decayed
 
 
-def weight_kernel(base_o, base_t, own, back2, back4, back6, out, share):
-    yh, group = lax.axis_index("y_hi"), lax.axis_index("z_hi")
-    for k, grad in enumerate((own, back2, back4, back6)):
-        at = lax.rem(group - k + 4, 4)
-        rows = pl.ds(pl.multiple_of(at * 32, 32), 32)
-        source = pl.ds(pl.multiple_of(lax.rem(at, 2) * 32, 32), 32)
-        base = jnp.where(at // 2 == yh, base_o[source, :], base_t[source, :])
-        share[rows, :] = grad[...]
-        out[rows, :] = (base - learning_rate * grad[...].astype(F32)).astype(BF16)
+def weight_kernel(base_o, base_t, own, back1, back2, back3, out, share, terms):
+    yh, pair = lax.axis_index("y_hi"), lax.axis_index("z_hi")
+    for k, term in enumerate((own, back1, back2, back3)):
+        terms[lax.rem(pair - k + 4, 4)] = term[...]
+    grad = add32(*[terms[k] for k in range(4)]).astype(BF16)
+    share[...] = grad
+    step = learning_rate * grad.astype(F32)
+    first, second = base_o[...], base_t[...]
+    out[0:64, :] = (jnp.where(yh == 0, first, second) - step[0:64]).astype(BF16)
+    out[64:128, :] = (jnp.where(yh == 0, second, first) - step[64:128]).astype(BF16)
 
 
 def product_kernel(share, *refs):
-    acts, weights, (slots, left, right) = refs[:4], refs[4:12], refs[12:]
+    acts, weights, (slots, left, right) = refs[:2], refs[2:10], refs[10:]
     z0, c, x, y = lax.axis_index("z_lo"), lax.axis_index("core"), place_x(), place_y()
     for i in range(8):
         dc, k = i // 4, i % 4
@@ -373,17 +354,20 @@
         for j in range(NY):
             for dz in range(2):
                 first = dz * 256 + j * 64
-                left[first : first + 64, at] = acts[j][dz, :, cols]
-    for dz in range(2):
-        total = jnp.dot(
-            left[dz * 256 : (dz + 1) * 256, :], right[...], preferred_element_type=F32
-        ).astype(BF16)
+                left[first : first + 64, at] = acts[j // 2][j % 2, dz, :, cols]
+
+    def parity(dz, carry):
+        rows = pl.ds(pl.multiple_of(dz * 256, 256), 256)
+        total = jnp.dot(left[rows, :], right[...], preferred_element_type=F32).astype(BF16)
         for j in range(NY):
-            y_to = lax.rem(y - j + NY, NY)
-            slot = y_to * 2 + (z0 ^ dz)
+            y_to = y ^ j
+            slot = y_to * 2 + lax.rem(z0 + dz, 2)
             slots[slot, 0:64, :] = total[j * 64 : (j + 1) * 64]
-            rows = pl.ds(pl.multiple_of((y_to // 2) * 64, 64), 64)
-            slots[slot, 64:128, :] = share[rows, :]
+            share_rows = pl.ds(pl.multiple_of((y_to // 2) * 64, 64), 64)
+            slots[slot, 64:128, :] = share[share_rows, :]
+        return carry
+
+    lax.fori_loop(0, 2, parity, 0)
 
 
 def join_kernel(momentum, slots, new_momentum, next_out):
@@ -401,7 +385,7 @@
 
     og_t = send(out_grad, other_core)
     hid_o, hid_x = call(
-        halves_kernel, [hidden_act], [near((rows, HALF))] * 2, moved=4 * 2**20, limit=16
+        halves_kernel, [hidden_act], [near((HALF, rows))] * 2, moved=4 * 2**20, limit=16
     )
     hid_t = send(hid_x, other_core)
     own = (tile_list, tile_count, hid_o, out_grad)
@@ -441,7 +425,7 @@
 
     cut_a = cuts(0, own_a, left_a, right_a, shift_x)
     cut_b = cuts(1, own_b, left_b, right_b, shift_y)
-    cut_a, cut_b = lax.optimization_barrier((cut_a, cut_b))
+    cut_a, cut_b, acts_z, base_x = lax.optimization_barrier((cut_a, cut_b, acts_z, base_x))
 
     plane_a, plane_b = [cut_a[0]], [cut_b[0]]
     for k in (1, 3, 2):
@@ -451,17 +435,19 @@
         plane_kernel, plane_a + plane_b, [near((CHUNK, QUARTER))] * 2, moved=3 * 2**20
     )
     given = send(give, other_z)
-    pair = jnp.stack([acts, acts_z])
-    pair = after(pair, give)
-    acts_y = [pair] + [send(pair, shift_y(k)) for k in (1, 2, 3)]
-    base_t = send(after(base_x, give), other_y_hi)
-    groups = call(pair_kernel, [held(keep), given], [near((32, QUARTER))] * 4, moved=2**20)
-    grad = add32(groups[0], *[send(groups[k], shift_z(2 * k)) for k in (2, 1, 3)]).astype(BF16)
-    back = {k: send(grad, shift_z(k)) for k in (4, 2, 6)}
+    (pair_sum,) = call(
+        pair_kernel, [held(keep), given], [near((CHUNK, QUARTER))], moved=2**20
+    )
+    others = [send(pair_sum, shift_z(2 * k)) for k in (2, 1, 3)]
+    pair = after(jnp.stack([acts, acts_z]), pair_sum)
+    four = jnp.stack([pair, send(pair, other_y_lo)])
+    acts_y = [four, send(four, other_y_hi)]
+    base_t = send(after(base_x, pair_sum), other_y_hi)
     own_weight, share = call(
         weight_kernel,
-        [held(base_o), base_t, grad] + [back[k] for k in (2, 4, 6)],
+        [held(base_o), base_t, held(pair_sum)] + [others[i] for i in (1, 0, 2)],
         [near((CHUNK, QUARTER))] * 2,
+        [pltpu.VMEM((4, CHUNK, QUARTER), BF16)],
         moved=2**20,
     )
     weights = [own_weight] + [send(own_weight, shift_x(k)) for k in (1, 2, 3)]

time: 159 us -> 152 us (0.956)
  Pallas kernels: 40.4 us -> 31.3 us
  waiting for transfers between devices: 25.4 us -> 33.7 us
  starting transfers between devices: 62.9 us -> 56.9 us
    pallas_call x4, Pallas kernels: 34.6 us -> 24.4 us  [gradients(): pl.pallas_call(functools.partial(grad_kernel, offsets, own is not None, o...]
    ppermute x37 -> x33, waiting for transfers between devices: 25.4 us -> 33.7 us  [send(): return lax.ppermute(value, AXES, pairs)]
    ppermute x37 -> x33, starting transfers between devices: 62.9 us -> 56.9 us  [send(): return lax.ppermute(value, AXES, pairs)]
  transfers between devices with their start and end apart: 37 -> 33, of which waited for: 11 -> 11; matrix products, arithmetic and copies ran while one was open for 0% -> 0% of each run, Pallas kernels for 20% -> 15%
where the time goes in v2:
time: 152 us; the launch traced here: 151 us
  starting transfers between devices  56.9 us (37%)
  waiting for transfers between devices  33.7 us (22%)
  Pallas kernels  31.3 us (21%)
  blocking collectives  25.8 us (17%)
  local copies, waits for them, and re-layouts  2.76 us (2%)
    ppermute x33, starting transfers between devices, send(): return lax.ppermute(value, AXES, pairs)  56.9 us
    ppermute x33, waiting for transfers between devices, send(): return lax.ppermute(value, AXES, pairs)  33.7 us
    all_to_all x1, blocking collectives, local(): slots = lax.all_to_all(slots, GROUP, 0, 0)  25.8 us
    pallas_call x4, Pallas kernels, gradients(): pl.pallas_call(functools.partial(grad_kernel, offsets, own is not None, o...  24.4 us
    pallas_call x11, Pallas kernels, call(): pl.pallas_call(kernel, out_shape=outs, in_specs=[vmem()] * len(arrays), o...  6.87 us
  transfers between devices with their start and end apart: 33, of which 11 were waited for; matrix products, arithmetic and copies ran while one was open for 0% of the time, Pallas kernels for 15%

profile of v2, /device:TPU:1, one launch (start us, length us, event | category | flops | bytes accessed | tf_op | source)
XLA Modules:
  0.0 151.5 jit_solution(15187219639748396494)
XLA Ops:
  0.6 3.3 %collective-permute-start.3 = (bf16[768,3584]{1,0:T(8,128)(2,1)}, bf16[768,3584]{1,0:T(8,128)(2,1)S(1)}, u32[]{:S(2)}, u32[]{:S(2)}) collective-permute-start(bf16[768,3584]{1,0:T(8,128)(2,1)} %refs_3_.1), channel_id=1, source_target_pairs={{0,16},{1,17},{2,18},{3,19},{4,20},{5,21},{6,22},{7,23},{8,24},{9,... | collective-permute-start | bytes 16515080 | tf_op jit(solution)/shard_map/ppermute | solution.py:41
  8.5 4.8 %shard_map.90 = (bf16[128,3584]{1,0:T(8,128)(2,1)S(1)}, bf16[512,896]{1,0:T(8,128)(2,1)S(1)}) custom-call(s32[1,1,2,6]{3,2,1,0:T(2,128)S(1)} %copy-done.4, s32[1,1,2]{2,1,0:T(1,128)S(1)} %copy-done.5, bf16[512,768]{1,0:T(8,128)(2,1)S(1)} %get-tuple-element.49.refs_4_.refs_2_, bf16[768,3584]{1,0:T(8,128)(2,1)} %refs_3_.1), custom_call_target="tpu_custom_call" | custom-call | flops 704643072 | bytes 10485760 | tf_op jit(solution)/shard_map/pallas_call | solution.py:249
  14.0 3.4 %shard_map.91 = (bf16[64,3584]{1,0:T(8,128)(2,1)S(1)}, bf16[64,3584]{1,0:T(8,128)(2,1)S(1)}, bf16[256,896]{1,0:T(8,128)(2,1)S(1)}, bf16[256,896]{1,0:T(8,128)(2,1)S(1)}) custom-call(s32[1,1,2,6]{3,2,1,0:T(2,128)S(1)} %collective-permute-done.refs_2_.refs_0_, s32[1,1,2]{2,1,0:T(1,128)S(1)} %collective-permute-done.1.refs_3_.refs_1_, ...), custom_call_target="tpu_custom_call" | custom-call | flops 704643072 | bytes 10485760 | tf_op jit(solution)/shard_map/pallas_call | solution.py:249
  17.5 2.7 %collective-permute-start.5 = (bf16[64,3584]{1,0:T(8,128)(2,1)S(1)}, bf16[64,3584]{1,0:T(8,128)(2,1)S(1)}, u32[]{:S(2)}, u32[]{:S(2)}) collective-permute-start(bf16[64,3584]{1,0:T(8,128)(2,1)S(1)} %get-tuple-element.57), channel_id=1, source_target_pairs={{0,96},{1,97},{2,98},{3,99},{4,100},{5,101},{6,102},{7,103},{8,104... | collective-permute-start | bytes 1376264 | tf_op jit(solution)/shard_map/ppermute | solution.py:41
  20.2 2.7 %collective-permute-start.7 = (bf16[256,896]{1,0:T(8,128)(2,1)S(1)}, bf16[256,896]{1,0:T(8,128)(2,1)S(1)}, u32[]{:S(2)}, u32[]{:S(2)}) collective-permute-start(bf16[256,896]{1,0:T(8,128)(2,1)S(1)} %get-tuple-element.61), channel_id=1, source_target_pairs={{0,136},{1,137},{2,138},{3,139},{4,140},{5,141},{6,142},{7,143},{8... | collective-permute-start | bytes 1376264 | tf_op jit(solution)/shard_map/ppermute | solution.py:41
  22.8 9.9 %shard_map.89 = (bf16[128,3584]{1,0:T(8,128)(2,1)S(1)}, bf16[128,3584]{1,0:T(8,128)(2,1)S(1)}, bf16[512,896]{1,0:T(8,128)(2,1)S(1)}, bf16[512,896]{1,0:T(8,128)(2,1)S(1)}) custom-call(s32[1,1,2,6]{3,2,1,0:T(2,128)S(1)} %copy-done.4, s32[1,1,2]{2,1,0:T(1,128)S(1)} %copy-done.5, s32[1,1,2,6]{3,2,1,0:T(2,128)S(1)} %collective-permute-done.refs_2_.refs_0_, ...), custom_call_target="tpu_custom_call" | custom-call | flops 2818572288 | bytes 20971520 | tf_op jit(solution)/shard_map/pallas_call | solution.py:249
  33.4 2.7 %collective-permute-start.9 = (bf16[128,3584]{1,0:T(8,128)(2,1)S(1)}, bf16[128,3584]{1,0:T(8,128)(2,1)S(1)}, u32[]{:S(2)}, u32[]{:S(2)}) collective-permute-start(bf16[128,3584]{1,0:T(8,128)(2,1)S(1)} %get-tuple-element.63), channel_id=1, source_target_pairs={{0,96},{1,97},{2,98},{3,99},{4,100},{5,101},{6,102},{7,103},{8,104... | collective-permute-start | bytes 2752520 | tf_op jit(solution)/shard_map/ppermute | solution.py:41
  36.1 2.7 %collective-permute-start.11 = (bf16[512,896]{1,0:T(8,128)(2,1)S(1)}, bf16[512,896]{1,0:T(8,128)(2,1)S(1)}, u32[]{:S(2)}, u32[]{:S(2)}) collective-permute-start(bf16[512,896]{1,0:T(8,128)(2,1)S(1)} %get-tuple-element.70), channel_id=1, source_target_pairs={{0,136},{1,137},{2,138},{3,139},{4,140},{5,141},{6,142},{7,143},{8... | collective-permute-start | bytes 2752520 | tf_op jit(solution)/shard_map/ppermute | solution.py:41
  39.1 6.3 %shard_map.88 = (bf16[128,3584]{1,0:T(8,128)(2,1)S(1)}, bf16[512,896]{1,0:T(8,128)(2,1)S(1)}) custom-call(s32[1,1,2,6]{3,2,1,0:T(2,128)S(1)} %copy-done.4, s32[1,1,2]{2,1,0:T(1,128)S(1)} %copy-done.5, s32[1,1,2,6]{3,2,1,0:T(2,128)S(1)} %collective-permute-done.refs_2_.refs_0_, s32[1,1,2]{2,1,0:T(1,128)S(1)} %collective-permute-done.1.refs_3_.refs_1_, ...), custom_call_target="tpu_custom_call" | custom-call | flops 1409286144 | bytes 16777216 | tf_op jit(solution)/shard_map/pallas_call | solution.py:249
  45.4 9.5 %collective-permute-done.8.left = bf16[128,3584]{1,0:T(8,128)(2,1)S(1)} collective-permute-done((bf16[128,3584]{1,0:T(8,128)(2,1)S(1)}, bf16[128,3584]{1,0:T(8,128)(2,1)S(1)}, u32[]{:S(2)}, u32[]{:S(2)}) %collective-permute-start.8) | collective-permute-done | bytes 917536 | tf_op jit(solution)/shard_map/ppermute | solution.py:41
  57.5 2.7 %collective-permute-start.14 = (bf16[128,896]{1,0:T(8,128)(2,1)S(1)}, bf16[128,896]{1,0:T(8,128)(2,1)S(1)}, u32[]{:S(2)}, u32[]{:S(2)}) collective-permute-start(bf16[128,896]{1,0:T(8,128)(2,1)S(1)} %get-tuple-element.80), channel_id=1, source_target_pairs={{0,136},{1,137},{2,138},{3,139},{4,140},{5,141},{6,142},{7,143},{8... | collective-permute-start | bytes 688136 | tf_op jit(solution)/shard_map/ppermute | solution.py:41
  61.1 2.7 %collective-permute-start.17 = (bf16[128,896]{1,0:T(8,128)(2,1)S(1)}, bf16[128,896]{1,0:T(8,128)(2,1)S(1)}, u32[]{:S(2)}, u32[]{:S(2)}) collective-permute-start(bf16[128,896]{1,0:T(8,128)(2,1)S(1)} %get-tuple-element.84), channel_id=1, source_target_pairs={{0,96},{1,97},{2,98},{3,99},{4,100},{5,101},{6,102},{7,103},{8,104... | collective-permute-start | bytes 688136 | tf_op jit(solution)/shard_map/ppermute | solution.py:41
  65.0 3.0 %collective-permute-done.15.refs_3_ = bf16[128,896]{1,0:T(8,128)(2,1)S(1)} collective-permute-done((bf16[128,896]{1,0:T(8,128)(2,1)S(1)}, bf16[128,896]{1,0:T(8,128)(2,1)S(1)}, u32[]{:S(2)}, u32[]{:S(2)}) %collective-permute-start.15) | collective-permute-done | bytes 229408 | tf_op jit(solution)/shard_map/ppermute | solution.py:41
  69.3 3.2 %collective-permute-done.18.refs_7_ = bf16[128,896]{1,0:T(8,128)(2,1)S(1)} collective-permute-done((bf16[128,896]{1,0:T(8,128)(2,1)S(1)}, bf16[128,896]{1,0:T(8,128)(2,1)S(1)}, u32[]{:S(2)}, u32[]{:S(2)}) %collective-permute-start.18) | collective-permute-done | bytes 229408 | tf_op jit(solution)/shard_map/ppermute | solution.py:41
  72.9 4.8 %collective-permute-done.19.given = bf16[128,896]{1,0:T(8,128)(2,1)S(1)} collective-permute-done((bf16[128,896]{1,0:T(8,128)(2,1)S(1)}, bf16[128,896]{1,0:T(8,128)(2,1)S(1)}, u32[]{:S(2)}, u32[]{:S(2)}) %collective-permute-start.19) | collective-permute-done | bytes 229408 | tf_op jit(solution)/shard_map/ppermute | solution.py:41
  80.2 4.1 %collective-permute-start.23 = (bf16[128,896]{1,0:T(8,128)(2,1)S(1)}, bf16[128,896]{1,0:T(8,128)(2,1)S(1)}, u32[]{:S(2)}, u32[]{:S(2)}) collective-permute-start(bf16[128,896]{1,0:T(8,128)(2,1)S(1)} %shard_map.97.own), channel_id=1, source_target_pairs={{0,6},{1,7},{2,0},{3,1},{4,2},{5,3},{6,4},{7,5},{8,14},{9,15},{10,... | collective-permute-start | bytes 688136 | tf_op jit(solution)/shard_map/ppermute | solution.py:41
  85.2 2.4 %collective-permute-start.21 = (bf16[128,896]{1,0:T(8,128)(2,1)S(1)}, bf16[128,896]{1,0:T(8,128)(2,1)S(1)}, u32[]{:S(2)}, u32[]{:S(2)}) collective-permute-start(bf16[128,896]{1,0:T(8,128)(2,1)S(1)} %shard_map.97.own), channel_id=1, source_target_pairs={{0,2},{1,3},{2,4},{3,5},{4,6},{5,7},{6,0},{7,1},{8,10},{9,11},{10,... | collective-permute-start | bytes 688136 | tf_op jit(solution)/shard_map/ppermute | solution.py:41
  89.4 5.5 %collective-permute-done.23.back3 = bf16[128,896]{1,0:T(8,128)(2,1)S(1)} collective-permute-done((bf16[128,896]{1,0:T(8,128)(2,1)S(1)}, bf16[128,896]{1,0:T(8,128)(2,1)S(1)}, u32[]{:S(2)}, u32[]{:S(2)}) %collective-permute-start.23) | collective-permute-done | bytes 229408 | tf_op jit(solution)/shard_map/ppermute | solution.py:41
  97.2 5.3 %collective-permute-start.27 = (bf16[128,896]{1,0:T(8,128)(2,1)S(1)}, bf16[128,896]{1,0:T(8,128)(2,1)S(1)}, u32[]{:S(2)}, u32[]{:S(2)}) collective-permute-start(bf16[128,896]{1,0:T(8,128)(2,1)S(1)} %get-tuple-element.93.refs_2_), channel_id=1, source_target_pairs={{0,64},{1,65},{2,66},{3,67},{4,68},{5,69},{6,70},{7,71},{8,72},{9,... | collective-permute-start | bytes 688136 | tf_op jit(solution)/shard_map/ppermute | solution.py:41
  102.5 9.3 %collective-permute-start.29 = (bf16[128,896]{1,0:T(8,128)(2,1)S(1)}, bf16[128,896]{1,0:T(8,128)(2,1)S(1)}, u32[]{:S(2)}, u32[]{:S(2)}) collective-permute-start(bf16[128,896]{1,0:T(8,128)(2,1)S(1)} %get-tuple-element.93.refs_2_), channel_id=1, source_target_pairs={{0,16},{1,17},{2,18},{3,19},{4,20},{5,21},{6,22},{7,23},{8,24},{9,... | collective-permute-start | bytes 688136 | tf_op jit(solution)/shard_map/ppermute | solution.py:41
  111.9 5.0 %collective-permute-start.32 = (bf16[128,896]{1,0:T(8,128)(2,1)S(1)}, bf16[128,896]{1,0:T(8,128)(2,1)S(1)}, u32[]{:S(2)}, u32[]{:S(2)}) collective-permute-start(bf16[128,896]{1,0:T(8,128)(2,1)S(1)} %collective-permute-done.28.refs_5_), channel_id=1, source_target_pairs={{0,16},{1,17},{2,18},{3,19},{4,20},{5,21},{6,22},{7,23},{8,24},{9,... | collective-permute-start | bytes 688136 | tf_op jit(solution)/shard_map/ppermute | solution.py:41
  118.5 2.4 %collective-permute-start.30 = (bf16[128,896]{1,0:T(8,128)(2,1)S(1)}, bf16[128,896]{1,0:T(8,128)(2,1)S(1)}, u32[]{:S(2)}, u32[]{:S(2)}) collective-permute-start(bf16[128,896]{1,0:T(8,128)(2,1)S(1)} %collective-permute-done.26.refs_3_), channel_id=1, source_target_pairs={{0,16},{1,17},{2,18},{3,19},{4,20},{5,21},{6,22},{7,23},{8,24},{9,... | collective-permute-start | bytes 688136 | tf_op jit(solution)/shard_map/ppermute | solution.py:41
  122.0 1.9 %shard_map.99 = bf16[8,128,896]{2,1,0:T(8,128)(2,1)S(1)} custom-call(bf16[128,896]{1,0:T(8,128)(2,1)S(1)} %get-tuple-element.89.share, bf16[2,2,64,1024]{3,2,1,0:T(8,128)(2,1)S(1)} %pad_maximum_fusion.refs_0_, bf16[2,2,64,1024]{3,2,1,0:T(8,128)(2,1)S(1)} %collective-permute-done.25.refs_1_, bf16[128,896]{1,0:T(8,128)(2,1)S(1)} %get-tuple-element.93.refs_2_, ...), custom_call_target="tpu_custom_call" | custom-call | flops 939524096 | bytes 4194304 | tf_op jit(solution)/shard_map/pallas_call | solution.py:97
  123.9 25.8 %all_to_all.5.slots = bf16[8,128,896]{2,1,0:T(8,128)(2,1)S(1)} all-to-all(bf16[8,128,896]{2,1,0:T(8,128)(2,1)S(1)} %shard_map.99), channel_id=1, replica_groups=mesh['y_hi'=2,'x'=4,'core'=2,'y_lo'=2,'z_hi'=4,'z_lo'=2] {'y_hi','y_lo',..., dimensions={0} | all-to-all | bytes 3670016 | tf_op jit(solution)/shard_map/all_to_all | solution.py:463
  (72 shorter events, 24.6 us)
Async XLA Ops:
  0.6 13.3 %collective-permute-start.3 = (bf16[768,3584]{1,0:T(8,128)(2,1)}, bf16[768,3584]{1,0:T(8,128)(2,1)S(1)}, u32[]{:S(2)}, u32[]{:S(2)}) collective-permute-start(bf16[768,3584]{1,0:T(8,128)(2,1)} %refs_3_.1), channel_id=1, source_target_pairs={{0,16},{1,17},{2,18},{3,19},{4,20},{5,21},{6,22},{7,23},{8,24},{9,... | collective-permute-start | bytes 16515080 | tf_op jit(solution)/shard_map/ppermute | solution.py:41
  17.4 15.3 %collective-permute-start.4 = (bf16[64,3584]{1,0:T(8,128)(2,1)S(1)}, bf16[64,3584]{1,0:T(8,128)(2,1)S(1)}, u32[]{:S(2)}, u32[]{:S(2)}) collective-permute-start(bf16[64,3584]{1,0:T(8,128)(2,1)S(1)} %get-tuple-element.56), channel_id=1, source_target_pairs={{0,32},{1,33},{2,34},{3,35},{4,36},{5,37},{6,38},{7,39},{8,40},{9,... | collective-permute-start | bytes 1376264 | tf_op jit(solution)/shard_map/ppermute | solution.py:41
  17.5 15.3 %collective-permute-start.5 = (bf16[64,3584]{1,0:T(8,128)(2,1)S(1)}, bf16[64,3584]{1,0:T(8,128)(2,1)S(1)}, u32[]{:S(2)}, u32[]{:S(2)}) collective-permute-start(bf16[64,3584]{1,0:T(8,128)(2,1)S(1)} %get-tuple-element.57), channel_id=1, source_target_pairs={{0,96},{1,97},{2,98},{3,99},{4,100},{5,101},{6,102},{7,103},{8,104... | collective-permute-start | bytes 1376264 | tf_op jit(solution)/shard_map/ppermute | solution.py:41
  20.1 12.6 %collective-permute-start.6 = (bf16[256,896]{1,0:T(8,128)(2,1)S(1)}, bf16[256,896]{1,0:T(8,128)(2,1)S(1)}, u32[]{:S(2)}, u32[]{:S(2)}) collective-permute-start(bf16[256,896]{1,0:T(8,128)(2,1)S(1)} %get-tuple-element.60), channel_id=1, source_target_pairs={{0,8},{1,9},{2,10},{3,11},{4,12},{5,13},{6,14},{7,15},{8,128},{9,1... | collective-permute-start | bytes 1376264 | tf_op jit(solution)/shard_map/ppermute | solution.py:41
  20.2 12.6 %collective-permute-start.7 = (bf16[256,896]{1,0:T(8,128)(2,1)S(1)}, bf16[256,896]{1,0:T(8,128)(2,1)S(1)}, u32[]{:S(2)}, u32[]{:S(2)}) collective-permute-start(bf16[256,896]{1,0:T(8,128)(2,1)S(1)} %get-tuple-element.61), channel_id=1, source_target_pairs={{0,136},{1,137},{2,138},{3,139},{4,140},{5,141},{6,142},{7,143},{8... | collective-permute-start | bytes 1376264 | tf_op jit(solution)/shard_map/ppermute | solution.py:41
  33.3 21.6 %collective-permute-start.8 = (bf16[128,3584]{1,0:T(8,128)(2,1)S(1)}, bf16[128,3584]{1,0:T(8,128)(2,1)S(1)}, u32[]{:S(2)}, u32[]{:S(2)}) collective-permute-start(bf16[128,3584]{1,0:T(8,128)(2,1)S(1)} %get-tuple-element.62), channel_id=1, source_target_pairs={{0,32},{1,33},{2,34},{3,35},{4,36},{5,37},{6,38},{7,39},{8,40},{9,... | collective-permute-start | bytes 2752520 | tf_op jit(solution)/shard_map/ppermute | solution.py:41
  33.4 21.5 %collective-permute-start.9 = (bf16[128,3584]{1,0:T(8,128)(2,1)S(1)}, bf16[128,3584]{1,0:T(8,128)(2,1)S(1)}, u32[]{:S(2)}, u32[]{:S(2)}) collective-permute-start(bf16[128,3584]{1,0:T(8,128)(2,1)S(1)} %get-tuple-element.63), channel_id=1, source_target_pairs={{0,96},{1,97},{2,98},{3,99},{4,100},{5,101},{6,102},{7,103},{8,104... | collective-permute-start | bytes 2752520 | tf_op jit(solution)/shard_map/ppermute | solution.py:41
  36.1 21.0 %collective-permute-start.10 = (bf16[512,896]{1,0:T(8,128)(2,1)S(1)}, bf16[512,896]{1,0:T(8,128)(2,1)S(1)}, u32[]{:S(2)}, u32[]{:S(2)}) collective-permute-start(bf16[512,896]{1,0:T(8,128)(2,1)S(1)} %get-tuple-element.69), channel_id=1, source_target_pairs={{0,8},{1,9},{2,10},{3,11},{4,12},{5,13},{6,14},{7,15},{8,128},{9,1... | collective-permute-start | bytes 2752520 | tf_op jit(solution)/shard_map/ppermute | solution.py:41
  36.1 21.0 %collective-permute-start.11 = (bf16[512,896]{1,0:T(8,128)(2,1)S(1)}, bf16[512,896]{1,0:T(8,128)(2,1)S(1)}, u32[]{:S(2)}, u32[]{:S(2)}) collective-permute-start(bf16[512,896]{1,0:T(8,128)(2,1)S(1)} %get-tuple-element.70), channel_id=1, source_target_pairs={{0,136},{1,137},{2,138},{3,139},{4,140},{5,141},{6,142},{7,143},{8... | collective-permute-start | bytes 2752520 | tf_op jit(solution)/shard_map/ppermute | solution.py:41
  38.9 18.5 %collective-permute-start.12 = (bf16[64,1024]{1,0:T(8,128)(2,1)S(1)}, bf16[64,1024]{1,0:T(8,128)(2,1)S(1)}, u32[]{:S(2)}, u32[]{:S(2)}) collective-permute-start(bf16[64,1024]{1,0:T(8,128)(2,1)S(1)} %get-tuple-element.75), channel_id=1, source_target_pairs={{0,1},{1,0},{2,3},{3,2},{4,5},{5,4},{6,7},{7,6},{8,9},{9,8},{10,11... | collective-permute-start | bytes 393224 | tf_op jit(solution)/shard_map/ppermute | solution.py:41
  60.1 7.9 %collective-permute-start.15 = (bf16[128,896]{1,0:T(8,128)(2,1)S(1)}, bf16[128,896]{1,0:T(8,128)(2,1)S(1)}, u32[]{:S(2)}, u32[]{:S(2)}) collective-permute-start(bf16[128,896]{1,0:T(8,128)(2,1)S(1)} %get-tuple-element.81), channel_id=1, source_target_pairs={{0,128},{1,129},{2,130},{3,131},{4,132},{5,133},{6,134},{7,135},{8... | collective-permute-start | bytes 688136 | tf_op jit(solution)/shard_map/ppermute | solution.py:41
  61.1 8.2 %collective-permute-start.17 = (bf16[128,896]{1,0:T(8,128)(2,1)S(1)}, bf16[128,896]{1,0:T(8,128)(2,1)S(1)}, u32[]{:S(2)}, u32[]{:S(2)}) collective-permute-start(bf16[128,896]{1,0:T(8,128)(2,1)S(1)} %get-tuple-element.84), channel_id=1, source_target_pairs={{0,96},{1,97},{2,98},{3,99},{4,100},{5,101},{6,102},{7,103},{8,104... | collective-permute-start | bytes 688136 | tf_op jit(solution)/shard_map/ppermute | solution.py:41
  63.7 8.8 %collective-permute-start.18 = (bf16[128,896]{1,0:T(8,128)(2,1)S(1)}, bf16[128,896]{1,0:T(8,128)(2,1)S(1)}, u32[]{:S(2)}, u32[]{:S(2)}) collective-permute-start(bf16[128,896]{1,0:T(8,128)(2,1)S(1)} %get-tuple-element.85), channel_id=1, source_target_pairs={{0,64},{1,65},{2,66},{3,67},{4,68},{5,69},{6,70},{7,71},{8,72},{9,... | collective-permute-start | bytes 688136 | tf_op jit(solution)/shard_map/ppermute | solution.py:41
  77.8 9.8 %collective-permute-start.24 = (bf16[2,64,1024]{2,1,0:T(8,128)(2,1)S(1)}, bf16[2,64,1024]{2,1,0:T(8,128)(2,1)S(1)}, u32[]{:S(2)}, u32[]{:S(2)}) collective-permute-start(bf16[2,64,1024]{2,1,0:T(8,128)(2,1)S(1)} %pad_maximum_fusion.1), channel_id=1, source_target_pairs={{0,8},{1,9},{2,10},{3,11},{4,12},{5,13},{6,14},{7,15},{8,0},{9,1},... | collective-permute-start | bytes 786440 | tf_op jit(solution)/shard_map/ppermute | solution.py:41
  78.7 10.7 %collective-permute-start.20 = (f32[64,896]{1,0:T(8,128)S(1)}, f32[64,896]{1,0:T(8,128)S(1)}, u32[]{:S(2)}, u32[]{:S(2)}) collective-permute-start(f32[64,896]{1,0:T(8,128)S(1)} %get-tuple-element.88), channel_id=1, source_target_pairs={{0,128},{1,129},{2,130},{3,131},{4,132},{5,133},{6,134},{7,135},{8... | collective-permute-start | bytes 688136 | tf_op jit(solution)/shard_map/ppermute | solution.py:41
  80.2 14.6 %collective-permute-start.23 = (bf16[128,896]{1,0:T(8,128)(2,1)S(1)}, bf16[128,896]{1,0:T(8,128)(2,1)S(1)}, u32[]{:S(2)}, u32[]{:S(2)}) collective-permute-start(bf16[128,896]{1,0:T(8,128)(2,1)S(1)} %shard_map.97.own), channel_id=1, source_target_pairs={{0,6},{1,7},{2,0},{3,1},{4,2},{5,3},{6,4},{7,5},{8,14},{9,15},{10,... | collective-permute-start | bytes 688136 | tf_op jit(solution)/shard_map/ppermute | solution.py:41
  84.3 12.1 %collective-permute-start.22 = (bf16[128,896]{1,0:T(8,128)(2,1)S(1)}, bf16[128,896]{1,0:T(8,128)(2,1)S(1)}, u32[]{:S(2)}, u32[]{:S(2)}) collective-permute-start(bf16[128,896]{1,0:T(8,128)(2,1)S(1)} %shard_map.97.own), channel_id=1, source_target_pairs={{0,4},{1,5},{2,6},{3,7},{4,0},{5,1},{6,2},{7,3},{8,12},{9,13},{10,... | collective-permute-start | bytes 688136 | tf_op jit(solution)/shard_map/ppermute | solution.py:41
  85.2 11.1 %collective-permute-start.21 = (bf16[128,896]{1,0:T(8,128)(2,1)S(1)}, bf16[128,896]{1,0:T(8,128)(2,1)S(1)}, u32[]{:S(2)}, u32[]{:S(2)}) collective-permute-start(bf16[128,896]{1,0:T(8,128)(2,1)S(1)} %shard_map.97.own), channel_id=1, source_target_pairs={{0,2},{1,3},{2,4},{3,5},{4,6},{5,7},{6,0},{7,1},{8,10},{9,11},{10,... | collective-permute-start | bytes 688136 | tf_op jit(solution)/shard_map/ppermute | solution.py:41
  87.7 34.3 %collective-permute-start.25 = (bf16[2,2,64,1024]{3,2,1,0:T(8,128)(2,1)S(1)}, bf16[2,2,64,1024]{3,2,1,0:T(8,128)(2,1)S(1)}, u32[]{:S(2)}, u32[]{:S(2)}) collective-permute-start(bf16[2,2,64,1024]{3,2,1,0:T(8,128)(2,1)S(1)} %pad_maximum_fusion.refs_0_), channel_id=1, source_target_pairs={{0,128},{1,129},{2,130},{3,131},{4,132},{5,133},{6,134},{7,135},{8... | collective-permute-start | bytes 1572872 | tf_op jit(solution)/shard_map/ppermute | solution.py:41
  96.8 15.0 %collective-permute-start.28 = (bf16[128,896]{1,0:T(8,128)(2,1)S(1)}, bf16[128,896]{1,0:T(8,128)(2,1)S(1)}, u32[]{:S(2)}, u32[]{:S(2)}) collective-permute-start(bf16[128,896]{1,0:T(8,128)(2,1)S(1)} %get-tuple-element.93.refs_2_), channel_id=1, source_target_pairs={{0,96},{1,97},{2,98},{3,99},{4,100},{5,101},{6,102},{7,103},{8,104... | collective-permute-start | bytes 688136 | tf_op jit(solution)/shard_map/ppermute | solution.py:41
  97.2 19.7 %collective-permute-start.27 = (bf16[128,896]{1,0:T(8,128)(2,1)S(1)}, bf16[128,896]{1,0:T(8,128)(2,1)S(1)}, u32[]{:S(2)}, u32[]{:S(2)}) collective-permute-start(bf16[128,896]{1,0:T(8,128)(2,1)S(1)} %get-tuple-element.93.refs_2_), channel_id=1, source_target_pairs={{0,64},{1,65},{2,66},{3,67},{4,68},{5,69},{6,70},{7,71},{8,72},{9,... | collective-permute-start | bytes 688136 | tf_op jit(solution)/shard_map/ppermute | solution.py:41
  102.5 16.0 %collective-permute-start.26 = (bf16[128,896]{1,0:T(8,128)(2,1)S(1)}, bf16[128,896]{1,0:T(8,128)(2,1)S(1)}, u32[]{:S(2)}, u32[]{:S(2)}) collective-permute-start(bf16[128,896]{1,0:T(8,128)(2,1)S(1)} %get-tuple-element.93.refs_2_), channel_id=1, source_target_pairs={{0,32},{1,33},{2,34},{3,35},{4,36},{5,37},{6,38},{7,39},{8,40},{9,... | collective-permute-start | bytes 688136 | tf_op jit(solution)/shard_map/ppermute | solution.py:41
  102.5 18.4 %collective-permute-start.29 = (bf16[128,896]{1,0:T(8,128)(2,1)S(1)}, bf16[128,896]{1,0:T(8,128)(2,1)S(1)}, u32[]{:S(2)}, u32[]{:S(2)}) collective-permute-start(bf16[128,896]{1,0:T(8,128)(2,1)S(1)} %get-tuple-element.93.refs_2_), channel_id=1, source_target_pairs={{0,16},{1,17},{2,18},{3,19},{4,20},{5,21},{6,22},{7,23},{8,24},{9,... | collective-permute-start | bytes 688136 | tf_op jit(solution)/shard_map/ppermute | solution.py:41
  111.9 9.0 %collective-permute-start.32 = (bf16[128,896]{1,0:T(8,128)(2,1)S(1)}, bf16[128,896]{1,0:T(8,128)(2,1)S(1)}, u32[]{:S(2)}, u32[]{:S(2)}) collective-permute-start(bf16[128,896]{1,0:T(8,128)(2,1)S(1)} %collective-permute-done.28.refs_5_), channel_id=1, source_target_pairs={{0,16},{1,17},{2,18},{3,19},{4,20},{5,21},{6,22},{7,23},{8,24},{9,... | collective-permute-start | bytes 688136 | tf_op jit(solution)/shard_map/ppermute | solution.py:41
  (15 other events, 75.5 us)

commit v3 on v2

--- a/solution.py
+++ b/solution.py
@@ -428,9 +428,8 @@
     cut_a, cut_b, acts_z, base_x = lax.optimization_barrier((cut_a, cut_b, acts_z, base_x))
 
     plane_a, plane_b = [cut_a[0]], [cut_b[0]]
-    for k in (1, 3, 2):
-        plane_a.append(send(cut_a[k], shift_y(k)))
-        plane_b.append(send(cut_b[k], shift_x(k)))
+    plane_a += [send(cut_a[k], shift_y(k)) for k in (1, 2, 3)]
+    plane_b += [send(cut_b[k], shift_x(k)) for k in (2, 1, 3)]
     keep, give = call(
         plane_kernel, plane_a + plane_b, [near((CHUNK, QUARTER))] * 2, moved=3 * 2**20
     )

time: 152 us -> 153 us (level)
  starting transfers between devices: 56.9 us -> 50.1 us
  blocking collectives: 25.8 us -> 30.4 us
  waiting for transfers between devices: 33.7 us -> 37.1 us
    ppermute x33, starting transfers between devices: 56.9 us -> 50.1 us  [send(): return lax.ppermute(value, AXES, pairs)]
    all_to_all x1, blocking collectives: 25.8 us -> 30.4 us  [local(): slots = lax.all_to_all(slots, GROUP, 0, 0)]
    ppermute x33, waiting for transfers between devices: 33.7 us -> 37.1 us  [send(): return lax.ppermute(value, AXES, pairs)]
  transfers between devices with their start and end apart: 33 -> 33, of which waited for: 11 -> 10; matrix products, arithmetic and copies ran while one was open for 0% -> 0% of each run, Pallas kernels for 15% -> 15%
where the time goes in v3:
time: 153 us
  starting transfers between devices  50.1 us (33%)
  waiting for transfers between devices  37.1 us (24%)
  Pallas kernels  31.3 us (20%)
  blocking collectives  30.4 us (20%)
  local copies, waits for them, and re-layouts  2.76 us (2%)
    ppermute x33, starting transfers between devices, send(): return lax.ppermute(value, AXES, pairs)  50.1 us
    ppermute x33, waiting for transfers between devices, send(): return lax.ppermute(value, AXES, pairs)  37.1 us
    all_to_all x1, blocking collectives, local(): slots = lax.all_to_all(slots, GROUP, 0, 0)  30.4 us
    pallas_call x4, Pallas kernels, gradients(): pl.pallas_call(functools.partial(grad_kernel, offsets, own is not None, o...  24.4 us
    pallas_call x11, Pallas kernels, call(): pl.pallas_call(kernel, out_shape=outs, in_specs=[vmem()] * len(arrays), o...  6.88 us
  transfers between devices with their start and end apart: 33, of which 10 were waited for; matrix products, arithmetic and copies ran while one was open for 0% of the time, Pallas kernels for 15%

profile of v3, /device:TPU:1, one launch (start us, length us, event | category | flops | bytes accessed | tf_op | source)
XLA Modules:
  0.0 152.7 jit_solution(3372373817124736269)
XLA Ops:
  0.6 3.3 %collective-permute-start.3 = (bf16[768,3584]{1,0:T(8,128)(2,1)}, bf16[768,3584]{1,0:T(8,128)(2,1)S(1)}, u32[]{:S(2)}, u32[]{:S(2)}) collective-permute-start(bf16[768,3584]{1,0:T(8,128)(2,1)} %refs_3_.1), channel_id=1, source_target_pairs={{0,16},{1,17},{2,18},{3,19},{4,20},{5,21},{6,22},{7,23},{8,24},{9,... | collective-permute-start | bytes 16515080 | tf_op jit(solution)/shard_map/ppermute | solution.py:41
  8.5 4.8 %shard_map.90 = (bf16[128,3584]{1,0:T(8,128)(2,1)S(1)}, bf16[512,896]{1,0:T(8,128)(2,1)S(1)}) custom-call(s32[1,1,2,6]{3,2,1,0:T(2,128)S(1)} %copy-done.4, s32[1,1,2]{2,1,0:T(1,128)S(1)} %copy-done.5, bf16[512,768]{1,0:T(8,128)(2,1)S(1)} %get-tuple-element.49.refs_4_.refs_2_, bf16[768,3584]{1,0:T(8,128)(2,1)} %refs_3_.1), custom_call_target="tpu_custom_call" | custom-call | flops 704643072 | bytes 10485760 | tf_op jit(solution)/shard_map/pallas_call | solution.py:249
  14.0 3.4 %shard_map.91 = (bf16[64,3584]{1,0:T(8,128)(2,1)S(1)}, bf16[64,3584]{1,0:T(8,128)(2,1)S(1)}, bf16[256,896]{1,0:T(8,128)(2,1)S(1)}, bf16[256,896]{1,0:T(8,128)(2,1)S(1)}) custom-call(s32[1,1,2,6]{3,2,1,0:T(2,128)S(1)} %collective-permute-done.refs_2_.refs_0_, s32[1,1,2]{2,1,0:T(1,128)S(1)} %collective-permute-done.1.refs_3_.refs_1_, ...), custom_call_target="tpu_custom_call" | custom-call | flops 704643072 | bytes 10485760 | tf_op jit(solution)/shard_map/pallas_call | solution.py:249
  17.5 2.7 %collective-permute-start.5 = (bf16[64,3584]{1,0:T(8,128)(2,1)S(1)}, bf16[64,3584]{1,0:T(8,128)(2,1)S(1)}, u32[]{:S(2)}, u32[]{:S(2)}) collective-permute-start(bf16[64,3584]{1,0:T(8,128)(2,1)S(1)} %get-tuple-element.57), channel_id=1, source_target_pairs={{0,96},{1,97},{2,98},{3,99},{4,100},{5,101},{6,102},{7,103},{8,104... | collective-permute-start | bytes 1376264 | tf_op jit(solution)/shard_map/ppermute | solution.py:41
  20.2 2.7 %collective-permute-start.7 = (bf16[256,896]{1,0:T(8,128)(2,1)S(1)}, bf16[256,896]{1,0:T(8,128)(2,1)S(1)}, u32[]{:S(2)}, u32[]{:S(2)}) collective-permute-start(bf16[256,896]{1,0:T(8,128)(2,1)S(1)} %get-tuple-element.61), channel_id=1, source_target_pairs={{0,136},{1,137},{2,138},{3,139},{4,140},{5,141},{6,142},{7,143},{8... | collective-permute-start | bytes 1376264 | tf_op jit(solution)/shard_map/ppermute | solution.py:41
  22.8 9.9 %shard_map.89 = (bf16[128,3584]{1,0:T(8,128)(2,1)S(1)}, bf16[128,3584]{1,0:T(8,128)(2,1)S(1)}, bf16[512,896]{1,0:T(8,128)(2,1)S(1)}, bf16[512,896]{1,0:T(8,128)(2,1)S(1)}) custom-call(s32[1,1,2,6]{3,2,1,0:T(2,128)S(1)} %copy-done.4, s32[1,1,2]{2,1,0:T(1,128)S(1)} %copy-done.5, s32[1,1,2,6]{3,2,1,0:T(2,128)S(1)} %collective-permute-done.refs_2_.refs_0_, ...), custom_call_target="tpu_custom_call" | custom-call | flops 2818572288 | bytes 20971520 | tf_op jit(solution)/shard_map/pallas_call | solution.py:249
  33.4 2.7 %collective-permute-start.9 = (bf16[128,3584]{1,0:T(8,128)(2,1)S(1)}, bf16[128,3584]{1,0:T(8,128)(2,1)S(1)}, u32[]{:S(2)}, u32[]{:S(2)}) collective-permute-start(bf16[128,3584]{1,0:T(8,128)(2,1)S(1)} %get-tuple-element.63), channel_id=1, source_target_pairs={{0,96},{1,97},{2,98},{3,99},{4,100},{5,101},{6,102},{7,103},{8,104... | collective-permute-start | bytes 2752520 | tf_op jit(solution)/shard_map/ppermute | solution.py:41
  36.1 2.7 %collective-permute-start.11 = (bf16[512,896]{1,0:T(8,128)(2,1)S(1)}, bf16[512,896]{1,0:T(8,128)(2,1)S(1)}, u32[]{:S(2)}, u32[]{:S(2)}) collective-permute-start(bf16[512,896]{1,0:T(8,128)(2,1)S(1)} %get-tuple-element.70), channel_id=1, source_target_pairs={{0,136},{1,137},{2,138},{3,139},{4,140},{5,141},{6,142},{7,143},{8... | collective-permute-start | bytes 2752520 | tf_op jit(solution)/shard_map/ppermute | solution.py:41
  39.1 6.3 %shard_map.88 = (bf16[128,3584]{1,0:T(8,128)(2,1)S(1)}, bf16[512,896]{1,0:T(8,128)(2,1)S(1)}) custom-call(s32[1,1,2,6]{3,2,1,0:T(2,128)S(1)} %copy-done.4, s32[1,1,2]{2,1,0:T(1,128)S(1)} %copy-done.5, s32[1,1,2,6]{3,2,1,0:T(2,128)S(1)} %collective-permute-done.refs_2_.refs_0_, s32[1,1,2]{2,1,0:T(1,128)S(1)} %collective-permute-done.1.refs_3_.refs_1_, ...), custom_call_target="tpu_custom_call" | custom-call | flops 1409286144 | bytes 16777216 | tf_op jit(solution)/shard_map/pallas_call | solution.py:249
  45.4 9.5 %collective-permute-done.8.left = bf16[128,3584]{1,0:T(8,128)(2,1)S(1)} collective-permute-done((bf16[128,3584]{1,0:T(8,128)(2,1)S(1)}, bf16[128,3584]{1,0:T(8,128)(2,1)S(1)}, u32[]{:S(2)}, u32[]{:S(2)}) %collective-permute-start.8) | collective-permute-done | bytes 917536 | tf_op jit(solution)/shard_map/ppermute | solution.py:41
  57.5 3.6 %collective-permute-start.14 = (bf16[128,896]{1,0:T(8,128)(2,1)S(1)}, bf16[128,896]{1,0:T(8,128)(2,1)S(1)}, u32[]{:S(2)}, u32[]{:S(2)}) collective-permute-start(bf16[128,896]{1,0:T(8,128)(2,1)S(1)} %get-tuple-element.80), channel_id=1, source_target_pairs={{0,128},{1,129},{2,130},{3,131},{4,132},{5,133},{6,134},{7,135},{8... | collective-permute-start | bytes 688136 | tf_op jit(solution)/shard_map/ppermute | solution.py:41
  64.2 3.8 %collective-permute-done.14.refs_2_ = bf16[128,896]{1,0:T(8,128)(2,1)S(1)} collective-permute-done((bf16[128,896]{1,0:T(8,128)(2,1)S(1)}, bf16[128,896]{1,0:T(8,128)(2,1)S(1)}, u32[]{:S(2)}, u32[]{:S(2)}) %collective-permute-start.14) | collective-permute-done | bytes 229408 | tf_op jit(solution)/shard_map/ppermute | solution.py:41
  68.1 1.8 %collective-permute-done.17.refs_6_ = bf16[128,896]{1,0:T(8,128)(2,1)S(1)} collective-permute-done((bf16[128,896]{1,0:T(8,128)(2,1)S(1)}, bf16[128,896]{1,0:T(8,128)(2,1)S(1)}, u32[]{:S(2)}, u32[]{:S(2)}) %collective-permute-start.17) | collective-permute-done | bytes 229408 | tf_op jit(solution)/shard_map/ppermute | solution.py:41
  70.5 4.9 %collective-permute-done.19.given = bf16[128,896]{1,0:T(8,128)(2,1)S(1)} collective-permute-done((bf16[128,896]{1,0:T(8,128)(2,1)S(1)}, bf16[128,896]{1,0:T(8,128)(2,1)S(1)}, u32[]{:S(2)}, u32[]{:S(2)}) %collective-permute-start.19) | collective-permute-done | bytes 229408 | tf_op jit(solution)/shard_map/ppermute | solution.py:41
  77.3 2.6 %collective-permute-start.20 = (f32[64,896]{1,0:T(8,128)S(1)}, f32[64,896]{1,0:T(8,128)S(1)}, u32[]{:S(2)}, u32[]{:S(2)}) collective-permute-start(f32[64,896]{1,0:T(8,128)S(1)} %get-tuple-element.88), channel_id=1, source_target_pairs={{0,128},{1,129},{2,130},{3,131},{4,132},{5,133},{6,134},{7,135},{8... | collective-permute-start | bytes 688136 | tf_op jit(solution)/shard_map/ppermute | solution.py:41
  79.9 4.4 %collective-permute-start.23 = (bf16[128,896]{1,0:T(8,128)(2,1)S(1)}, bf16[128,896]{1,0:T(8,128)(2,1)S(1)}, u32[]{:S(2)}, u32[]{:S(2)}) collective-permute-start(bf16[128,896]{1,0:T(8,128)(2,1)S(1)} %shard_map.97.own), channel_id=1, source_target_pairs={{0,6},{1,7},{2,0},{3,1},{4,2},{5,3},{6,4},{7,5},{8,14},{9,15},{10,... | collective-permute-start | bytes 688136 | tf_op jit(solution)/shard_map/ppermute | solution.py:41
  85.2 2.4 %collective-permute-start.21 = (bf16[128,896]{1,0:T(8,128)(2,1)S(1)}, bf16[128,896]{1,0:T(8,128)(2,1)S(1)}, u32[]{:S(2)}, u32[]{:S(2)}) collective-permute-start(bf16[128,896]{1,0:T(8,128)(2,1)S(1)} %shard_map.97.own), channel_id=1, source_target_pairs={{0,2},{1,3},{2,4},{3,5},{4,6},{5,7},{6,0},{7,1},{8,10},{9,11},{10,... | collective-permute-start | bytes 688136 | tf_op jit(solution)/shard_map/ppermute | solution.py:41
  88.2 8.3 %collective-permute-done.22.back2 = bf16[128,896]{1,0:T(8,128)(2,1)S(1)} collective-permute-done((bf16[128,896]{1,0:T(8,128)(2,1)S(1)}, bf16[128,896]{1,0:T(8,128)(2,1)S(1)}, u32[]{:S(2)}, u32[]{:S(2)}) %collective-permute-start.22) | collective-permute-done | bytes 229408 | tf_op jit(solution)/shard_map/ppermute | solution.py:41
  96.5 3.4 %collective-permute-done.21.back1 = bf16[128,896]{1,0:T(8,128)(2,1)S(1)} collective-permute-done((bf16[128,896]{1,0:T(8,128)(2,1)S(1)}, bf16[128,896]{1,0:T(8,128)(2,1)S(1)}, u32[]{:S(2)}, u32[]{:S(2)}) %collective-permute-start.21) | collective-permute-done | bytes 229408 | tf_op jit(solution)/shard_map/ppermute | solution.py:41
  101.9 8.0 %collective-permute-start.29 = (bf16[128,896]{1,0:T(8,128)(2,1)S(1)}, bf16[128,896]{1,0:T(8,128)(2,1)S(1)}, u32[]{:S(2)}, u32[]{:S(2)}) collective-permute-start(bf16[128,896]{1,0:T(8,128)(2,1)S(1)} %get-tuple-element.93.refs_2_), channel_id=1, source_target_pairs={{0,16},{1,17},{2,18},{3,19},{4,20},{5,21},{6,22},{7,23},{8,24},{9,... | collective-permute-start | bytes 688136 | tf_op jit(solution)/shard_map/ppermute | solution.py:41
  109.9 3.6 %collective-permute-start.32 = (bf16[128,896]{1,0:T(8,128)(2,1)S(1)}, bf16[128,896]{1,0:T(8,128)(2,1)S(1)}, u32[]{:S(2)}, u32[]{:S(2)}) collective-permute-start(bf16[128,896]{1,0:T(8,128)(2,1)S(1)} %collective-permute-done.28.refs_5_), channel_id=1, source_target_pairs={{0,16},{1,17},{2,18},{3,19},{4,20},{5,21},{6,22},{7,23},{8,24},{9,... | collective-permute-start | bytes 688136 | tf_op jit(solution)/shard_map/ppermute | solution.py:41
  115.1 2.4 %collective-permute-start.30 = (bf16[128,896]{1,0:T(8,128)(2,1)S(1)}, bf16[128,896]{1,0:T(8,128)(2,1)S(1)}, u32[]{:S(2)}, u32[]{:S(2)}) collective-permute-start(bf16[128,896]{1,0:T(8,128)(2,1)S(1)} %collective-permute-done.26.refs_3_), channel_id=1, source_target_pairs={{0,16},{1,17},{2,18},{3,19},{4,20},{5,21},{6,22},{7,23},{8,24},{9,... | collective-permute-start | bytes 688136 | tf_op jit(solution)/shard_map/ppermute | solution.py:41
  118.6 1.9 %shard_map.99 = bf16[8,128,896]{2,1,0:T(8,128)(2,1)S(1)} custom-call(bf16[128,896]{1,0:T(8,128)(2,1)S(1)} %get-tuple-element.89.share, bf16[2,2,64,1024]{3,2,1,0:T(8,128)(2,1)S(1)} %pad_maximum_fusion.refs_0_, bf16[2,2,64,1024]{3,2,1,0:T(8,128)(2,1)S(1)} %collective-permute-done.25.refs_1_, bf16[128,896]{1,0:T(8,128)(2,1)S(1)} %get-tuple-element.93.refs_2_, ...), custom_call_target="tpu_custom_call" | custom-call | flops 939524096 | bytes 4194304 | tf_op jit(solution)/shard_map/pallas_call | solution.py:97
  120.4 30.4 %all_to_all.5.slots = bf16[8,128,896]{2,1,0:T(8,128)(2,1)S(1)} all-to-all(bf16[8,128,896]{2,1,0:T(8,128)(2,1)S(1)} %shard_map.99), channel_id=1, replica_groups=mesh['y_hi'=2,'x'=4,'core'=2,'y_lo'=2,'z_hi'=4,'z_lo'=2] {'y_hi','y_lo',..., dimensions={0} | all-to-all | bytes 3670016 | tf_op jit(solution)/shard_map/all_to_all | solution.py:462
  (72 shorter events, 22.4 us)
Async XLA Ops:
  0.6 13.3 %collective-permute-start.3 = (bf16[768,3584]{1,0:T(8,128)(2,1)}, bf16[768,3584]{1,0:T(8,128)(2,1)S(1)}, u32[]{:S(2)}, u32[]{:S(2)}) collective-permute-start(bf16[768,3584]{1,0:T(8,128)(2,1)} %refs_3_.1), channel_id=1, source_target_pairs={{0,16},{1,17},{2,18},{3,19},{4,20},{5,21},{6,22},{7,23},{8,24},{9,... | collective-permute-start | bytes 16515080 | tf_op jit(solution)/shard_map/ppermute | solution.py:41
  6.5 7.5 %collective-permute-start.2 = (bf16[512,768]{1,0:T(8,128)(2,1)S(1)}, bf16[512,768]{1,0:T(8,128)(2,1)S(1)}, u32[]{:S(2)}, u32[]{:S(2)}) collective-permute-start(bf16[512,768]{1,0:T(8,128)(2,1)S(1)} %get-tuple-element.50), channel_id=1, source_target_pairs={{0,16},{1,17},{2,18},{3,19},{4,20},{5,21},{6,22},{7,23},{8,24},{9,... | collective-permute-start | bytes 2359304 | tf_op jit(solution)/shard_map/ppermute | solution.py:41
  17.4 15.3 %collective-permute-start.4 = (bf16[64,3584]{1,0:T(8,128)(2,1)S(1)}, bf16[64,3584]{1,0:T(8,128)(2,1)S(1)}, u32[]{:S(2)}, u32[]{:S(2)}) collective-permute-start(bf16[64,3584]{1,0:T(8,128)(2,1)S(1)} %get-tuple-element.56), channel_id=1, source_target_pairs={{0,32},{1,33},{2,34},{3,35},{4,36},{5,37},{6,38},{7,39},{8,40},{9,... | collective-permute-start | bytes 1376264 | tf_op jit(solution)/shard_map/ppermute | solution.py:41
  17.5 15.3 %collective-permute-start.5 = (bf16[64,3584]{1,0:T(8,128)(2,1)S(1)}, bf16[64,3584]{1,0:T(8,128)(2,1)S(1)}, u32[]{:S(2)}, u32[]{:S(2)}) collective-permute-start(bf16[64,3584]{1,0:T(8,128)(2,1)S(1)} %get-tuple-element.57), channel_id=1, source_target_pairs={{0,96},{1,97},{2,98},{3,99},{4,100},{5,101},{6,102},{7,103},{8,104... | collective-permute-start | bytes 1376264 | tf_op jit(solution)/shard_map/ppermute | solution.py:41
  20.1 12.6 %collective-permute-start.6 = (bf16[256,896]{1,0:T(8,128)(2,1)S(1)}, bf16[256,896]{1,0:T(8,128)(2,1)S(1)}, u32[]{:S(2)}, u32[]{:S(2)}) collective-permute-start(bf16[256,896]{1,0:T(8,128)(2,1)S(1)} %get-tuple-element.60), channel_id=1, source_target_pairs={{0,8},{1,9},{2,10},{3,11},{4,12},{5,13},{6,14},{7,15},{8,128},{9,1... | collective-permute-start | bytes 1376264 | tf_op jit(solution)/shard_map/ppermute | solution.py:41
  20.2 12.6 %collective-permute-start.7 = (bf16[256,896]{1,0:T(8,128)(2,1)S(1)}, bf16[256,896]{1,0:T(8,128)(2,1)S(1)}, u32[]{:S(2)}, u32[]{:S(2)}) collective-permute-start(bf16[256,896]{1,0:T(8,128)(2,1)S(1)} %get-tuple-element.61), channel_id=1, source_target_pairs={{0,136},{1,137},{2,138},{3,139},{4,140},{5,141},{6,142},{7,143},{8... | collective-permute-start | bytes 1376264 | tf_op jit(solution)/shard_map/ppermute | solution.py:41
  33.3 21.6 %collective-permute-start.8 = (bf16[128,3584]{1,0:T(8,128)(2,1)S(1)}, bf16[128,3584]{1,0:T(8,128)(2,1)S(1)}, u32[]{:S(2)}, u32[]{:S(2)}) collective-permute-start(bf16[128,3584]{1,0:T(8,128)(2,1)S(1)} %get-tuple-element.62), channel_id=1, source_target_pairs={{0,32},{1,33},{2,34},{3,35},{4,36},{5,37},{6,38},{7,39},{8,40},{9,... | collective-permute-start | bytes 2752520 | tf_op jit(solution)/shard_map/ppermute | solution.py:41
  33.4 21.5 %collective-permute-start.9 = (bf16[128,3584]{1,0:T(8,128)(2,1)S(1)}, bf16[128,3584]{1,0:T(8,128)(2,1)S(1)}, u32[]{:S(2)}, u32[]{:S(2)}) collective-permute-start(bf16[128,3584]{1,0:T(8,128)(2,1)S(1)} %get-tuple-element.63), channel_id=1, source_target_pairs={{0,96},{1,97},{2,98},{3,99},{4,100},{5,101},{6,102},{7,103},{8,104... | collective-permute-start | bytes 2752520 | tf_op jit(solution)/shard_map/ppermute | solution.py:41
  36.1 21.0 %collective-permute-start.10 = (bf16[512,896]{1,0:T(8,128)(2,1)S(1)}, bf16[512,896]{1,0:T(8,128)(2,1)S(1)}, u32[]{:S(2)}, u32[]{:S(2)}) collective-permute-start(bf16[512,896]{1,0:T(8,128)(2,1)S(1)} %get-tuple-element.69), channel_id=1, source_target_pairs={{0,8},{1,9},{2,10},{3,11},{4,12},{5,13},{6,14},{7,15},{8,128},{9,1... | collective-permute-start | bytes 2752520 | tf_op jit(solution)/shard_map/ppermute | solution.py:41
  36.1 21.0 %collective-permute-start.11 = (bf16[512,896]{1,0:T(8,128)(2,1)S(1)}, bf16[512,896]{1,0:T(8,128)(2,1)S(1)}, u32[]{:S(2)}, u32[]{:S(2)}) collective-permute-start(bf16[512,896]{1,0:T(8,128)(2,1)S(1)} %get-tuple-element.70), channel_id=1, source_target_pairs={{0,136},{1,137},{2,138},{3,139},{4,140},{5,141},{6,142},{7,143},{8... | collective-permute-start | bytes 2752520 | tf_op jit(solution)/shard_map/ppermute | solution.py:41
  38.9 18.5 %collective-permute-start.12 = (bf16[64,1024]{1,0:T(8,128)(2,1)S(1)}, bf16[64,1024]{1,0:T(8,128)(2,1)S(1)}, u32[]{:S(2)}, u32[]{:S(2)}) collective-permute-start(bf16[64,1024]{1,0:T(8,128)(2,1)S(1)} %get-tuple-element.75), channel_id=1, source_target_pairs={{0,1},{1,0},{2,3},{3,2},{4,5},{5,4},{6,7},{7,6},{8,9},{9,8},{10,11... | collective-permute-start | bytes 393224 | tf_op jit(solution)/shard_map/ppermute | solution.py:41
  57.5 10.5 %collective-permute-start.14 = (bf16[128,896]{1,0:T(8,128)(2,1)S(1)}, bf16[128,896]{1,0:T(8,128)(2,1)S(1)}, u32[]{:S(2)}, u32[]{:S(2)}) collective-permute-start(bf16[128,896]{1,0:T(8,128)(2,1)S(1)} %get-tuple-element.80), channel_id=1, source_target_pairs={{0,128},{1,129},{2,130},{3,131},{4,132},{5,133},{6,134},{7,135},{8... | collective-permute-start | bytes 688136 | tf_op jit(solution)/shard_map/ppermute | solution.py:41
  61.1 8.9 %collective-permute-start.17 = (bf16[128,896]{1,0:T(8,128)(2,1)S(1)}, bf16[128,896]{1,0:T(8,128)(2,1)S(1)}, u32[]{:S(2)}, u32[]{:S(2)}) collective-permute-start(bf16[128,896]{1,0:T(8,128)(2,1)S(1)} %get-tuple-element.84), channel_id=1, source_target_pairs={{0,32},{1,33},{2,34},{3,35},{4,36},{5,37},{6,38},{7,39},{8,40},{9,... | collective-permute-start | bytes 688136 | tf_op jit(solution)/shard_map/ppermute | solution.py:41
  75.5 12.1 %collective-permute-start.24 = (bf16[2,64,1024]{2,1,0:T(8,128)(2,1)S(1)}, bf16[2,64,1024]{2,1,0:T(8,128)(2,1)S(1)}, u32[]{:S(2)}, u32[]{:S(2)}) collective-permute-start(bf16[2,64,1024]{2,1,0:T(8,128)(2,1)S(1)} %pad_maximum_fusion.1), channel_id=1, source_target_pairs={{0,8},{1,9},{2,10},{3,11},{4,12},{5,13},{6,14},{7,15},{8,0},{9,1},... | collective-permute-start | bytes 786440 | tf_op jit(solution)/shard_map/ppermute | solution.py:41
  77.3 10.9 %collective-permute-start.20 = (f32[64,896]{1,0:T(8,128)S(1)}, f32[64,896]{1,0:T(8,128)S(1)}, u32[]{:S(2)}, u32[]{:S(2)}) collective-permute-start(f32[64,896]{1,0:T(8,128)S(1)} %get-tuple-element.88), channel_id=1, source_target_pairs={{0,128},{1,129},{2,130},{3,131},{4,132},{5,133},{6,134},{7,135},{8... | collective-permute-start | bytes 688136 | tf_op jit(solution)/shard_map/ppermute | solution.py:41
  79.9 8.3 %collective-permute-start.23 = (bf16[128,896]{1,0:T(8,128)(2,1)S(1)}, bf16[128,896]{1,0:T(8,128)(2,1)S(1)}, u32[]{:S(2)}, u32[]{:S(2)}) collective-permute-start(bf16[128,896]{1,0:T(8,128)(2,1)S(1)} %shard_map.97.own), channel_id=1, source_target_pairs={{0,6},{1,7},{2,0},{3,1},{4,2},{5,3},{6,4},{7,5},{8,14},{9,15},{10,... | collective-permute-start | bytes 688136 | tf_op jit(solution)/shard_map/ppermute | solution.py:41
  84.3 12.2 %collective-permute-start.22 = (bf16[128,896]{1,0:T(8,128)(2,1)S(1)}, bf16[128,896]{1,0:T(8,128)(2,1)S(1)}, u32[]{:S(2)}, u32[]{:S(2)}) collective-permute-start(bf16[128,896]{1,0:T(8,128)(2,1)S(1)} %shard_map.97.own), channel_id=1, source_target_pairs={{0,4},{1,5},{2,6},{3,7},{4,0},{5,1},{6,2},{7,3},{8,12},{9,13},{10,... | collective-permute-start | bytes 688136 | tf_op jit(solution)/shard_map/ppermute | solution.py:41
  85.2 14.7 %collective-permute-start.21 = (bf16[128,896]{1,0:T(8,128)(2,1)S(1)}, bf16[128,896]{1,0:T(8,128)(2,1)S(1)}, u32[]{:S(2)}, u32[]{:S(2)}) collective-permute-start(bf16[128,896]{1,0:T(8,128)(2,1)S(1)} %shard_map.97.own), channel_id=1, source_target_pairs={{0,2},{1,3},{2,4},{3,5},{4,6},{5,7},{6,0},{7,1},{8,10},{9,11},{10,... | collective-permute-start | bytes 688136 | tf_op jit(solution)/shard_map/ppermute | solution.py:41
  87.6 31.0 %collective-permute-start.25 = (bf16[2,2,64,1024]{3,2,1,0:T(8,128)(2,1)S(1)}, bf16[2,2,64,1024]{3,2,1,0:T(8,128)(2,1)S(1)}, u32[]{:S(2)}, u32[]{:S(2)}) collective-permute-start(bf16[2,2,64,1024]{3,2,1,0:T(8,128)(2,1)S(1)} %pad_maximum_fusion.refs_0_), channel_id=1, source_target_pairs={{0,128},{1,129},{2,130},{3,131},{4,132},{5,133},{6,134},{7,135},{8... | collective-permute-start | bytes 1572872 | tf_op jit(solution)/shard_map/ppermute | solution.py:41
  100.4 9.5 %collective-permute-start.28 = (bf16[128,896]{1,0:T(8,128)(2,1)S(1)}, bf16[128,896]{1,0:T(8,128)(2,1)S(1)}, u32[]{:S(2)}, u32[]{:S(2)}) collective-permute-start(bf16[128,896]{1,0:T(8,128)(2,1)S(1)} %get-tuple-element.93.refs_2_), channel_id=1, source_target_pairs={{0,96},{1,97},{2,98},{3,99},{4,100},{5,101},{6,102},{7,103},{8,104... | collective-permute-start | bytes 688136 | tf_op jit(solution)/shard_map/ppermute | solution.py:41
  100.5 13.0 %collective-permute-start.27 = (bf16[128,896]{1,0:T(8,128)(2,1)S(1)}, bf16[128,896]{1,0:T(8,128)(2,1)S(1)}, u32[]{:S(2)}, u32[]{:S(2)}) collective-permute-start(bf16[128,896]{1,0:T(8,128)(2,1)S(1)} %get-tuple-element.93.refs_2_), channel_id=1, source_target_pairs={{0,64},{1,65},{2,66},{3,67},{4,68},{5,69},{6,70},{7,71},{8,72},{9,... | collective-permute-start | bytes 688136 | tf_op jit(solution)/shard_map/ppermute | solution.py:41
  100.6 14.5 %collective-permute-start.26 = (bf16[128,896]{1,0:T(8,128)(2,1)S(1)}, bf16[128,896]{1,0:T(8,128)(2,1)S(1)}, u32[]{:S(2)}, u32[]{:S(2)}) collective-permute-start(bf16[128,896]{1,0:T(8,128)(2,1)S(1)} %get-tuple-element.93.refs_2_), channel_id=1, source_target_pairs={{0,32},{1,33},{2,34},{3,35},{4,36},{5,37},{6,38},{7,39},{8,40},{9,... | collective-permute-start | bytes 688136 | tf_op jit(solution)/shard_map/ppermute | solution.py:41
  101.9 15.5 %collective-permute-start.29 = (bf16[128,896]{1,0:T(8,128)(2,1)S(1)}, bf16[128,896]{1,0:T(8,128)(2,1)S(1)}, u32[]{:S(2)}, u32[]{:S(2)}) collective-permute-start(bf16[128,896]{1,0:T(8,128)(2,1)S(1)} %get-tuple-element.93.refs_2_), channel_id=1, source_target_pairs={{0,16},{1,17},{2,18},{3,19},{4,20},{5,21},{6,22},{7,23},{8,24},{9,... | collective-permute-start | bytes 688136 | tf_op jit(solution)/shard_map/ppermute | solution.py:41
  109.9 7.6 %collective-permute-start.32 = (bf16[128,896]{1,0:T(8,128)(2,1)S(1)}, bf16[128,896]{1,0:T(8,128)(2,1)S(1)}, u32[]{:S(2)}, u32[]{:S(2)}) collective-permute-start(bf16[128,896]{1,0:T(8,128)(2,1)S(1)} %collective-permute-done.28.refs_5_), channel_id=1, source_target_pairs={{0,16},{1,17},{2,18},{3,19},{4,20},{5,21},{6,22},{7,23},{8,24},{9,... | collective-permute-start | bytes 688136 | tf_op jit(solution)/shard_map/ppermute | solution.py:41
  (15 other events, 74.0 us)
